TPU v7x, 128 devices: a whole 4x4x4 slice. The times are simulated.
128 devices in a mesh: dp: 32 (over y, z, core), mp: 4 (over x).
Axes of the slice: x: 4, y: 4, z: 4, core: 2. Of those that a mesh axis runs over, the one named last changes fastest.
Arguments:
- layer_in: bfloat16 [8192, 2048], P('dp'), may hold values from -6 to 6
- cotangent: bfloat16 [8192, 2048], P('dp', 'mp'), may hold values from -6 to 6
- segments: int32 [8192], P('dp'), may hold values from 0 to 7, as said below
- adapters: int32 [8], replicated, may hold values from 0 to 7
- norm_one: float32 [2048], replicated, may hold values from 0.5 to 1.5
- norm_two: float32 [2048], replicated, may hold values from 0.5 to 1.5
- out_gain: float32 [128], replicated, may hold values from 0.5 to 1.5
- beta_bias: float32 [16], P('mp'), may hold values from -7.5 to 0
- conv_taps: bfloat16 [4, 3, 2048], P(None, None, 'mp'), may hold values from -3 to 3
- w_qkv: bfloat16 [2048, 3, 2048], P('dp', None, 'mp'), may hold values from -0.125 to 0.125
- w_beta: bfloat16 [2048, 16], P('dp', 'mp'), may hold values from -0.125 to 0.125
- w_out: bfloat16 [2048, 2048], P('mp', 'dp'), may hold values from -0.125 to 0.125
- w_gate_up: bfloat16 [2048, 2, 5632], P('dp', None, 'mp'), may hold values from -0.125 to 0.125
- w_down: bfloat16 [5632, 2048], P('mp', 'dp'), may hold values from -0.078125 to 0.078125
- a_in: bfloat16 [2048, 6, 128], P(('dp', 'mp')), may hold values from -0.125 to 0.125
- b_heads: bfloat16 [3, 128, 2048], P(None, 'dp', 'mp'), may hold values from -0.75 to 0.75
- b_beta: bfloat16 [128, 16], P('dp', 'mp'), may hold values from -0.75 to 0.75
- a_out: bfloat16 [2048, 128], P('mp', 'dp'), may hold values from -0.125 to 0.125
- b_ffn: bfloat16 [2, 128, 5632], P(None, 'dp', 'mp'), may hold values from -0.75 to 0.75
- a_down: bfloat16 [5632, 128], P('mp', 'dp'), may hold values from -0.078125 to 0.078125
- b_res: bfloat16 [2, 128, 2048], P(None, None, ('dp', 'mp')), may hold values from -0.75 to 0.75
Outputs:
- output: bfloat16 [8192, 2048], P('dp', 'mp')
- grad_input: float32 [8192, 2048], P('dp', 'mp')
- grad_a_in: float32 [2048, 6, 128], P(('dp', 'mp'))
- grad_b_heads: float32 [3, 128, 2048], P(None, 'dp', 'mp')
- grad_b_beta: float32 [128, 16], P('dp', 'mp')
- grad_a_out: float32 [2048, 128], P('mp', 'dp')
- grad_b_ffn: float32 [2, 128, 5632], P(None, 'dp', 'mp')
- grad_a_down: float32 [5632, 128], P('mp', 'dp')
- grad_b_res: float32 [2, 128, 2048], P(None, None, ('dp', 'mp'))
Inputs may be any that keep to these rules, and one draw needn't show every extreme that they name: `segments`: document numbers start at 0, never fall, and rise by one at every multiple of 8192 tokens and at 7 further places inside each packed sequence, never at the first token of an index of dp and one of them within the first 256 tokens of the sequence; a packed sequence spans 32 indices of dp.
All inputs are finite; a program needn't handle non-finite values.
Results may differ from a plain program's by a relative error of at most 0.03.
Values may be sent and summed in bfloat16 or wider, within the bound.
A program may use at most 256 MiB of HBM per device.

v0:
```python
import functools

import jax
import jax.numpy as jnp
from jax import lax
from jax.experimental import pallas as pl
from jax.experimental.pallas import tpu as pltpu
from jax.sharding import PartitionSpec as P

DH = 128
KW = 4
RANK = 16
HALO = 16
EPSILON = 1e-06
WIDE = jnp.float32
NARROW = jnp.bfloat16
MESH = pl.DeviceIdType.MESH
EXACT = lax.Precision.HIGHEST


def coords():
    place = lax.axis_index("dp")
    return place // 8, lax.rem(place // 2, 4), lax.rem(place, 2)


def place_of(y, z, c):
    return (y * 4 + z) * 2 + c


def moved(dy, dz, other_core=False):
    y, z, c = coords()
    return place_of(lax.rem(y + dy + 4, 4), lax.rem(z + dz + 4, 4), 1 - c if other_core else c)


def greet(dp_peers=(), mp_peers=()):
    barrier = pltpu.get_barrier_semaphore()
    for peer in dp_peers:
        pl.semaphore_signal(barrier, inc=1, device_id={"dp": peer}, device_id_type=MESH)
    for peer in mp_peers:
        pl.semaphore_signal(barrier, inc=1, device_id={"mp": peer}, device_id_type=MESH)
    pl.semaphore_wait(barrier, len(dp_peers) + len(mp_peers))


class Mailbox:
    def __init__(self, send, recv):
        self.send, self.recv, self.copies = send, recv, []

    def push(self, src, dst, **device):
        k = len(self.copies)
        copy = pltpu.make_async_remote_copy(
            src_ref=src,
            dst_ref=dst,
            send_sem=self.send.at[k],
            recv_sem=self.recv.at[k],
            device_id=device,
            device_id_type=MESH,
        )
        copy.start()
        self.copies.append(copy)
        return copy

    def drain(self):
        for copy in self.copies:
            copy.wait_send()


def gather_steps(box, own, out):
    me = moved(0, 0)
    half = own.shape[0] // 2
    quarter = half // 2
    sibling = moved(0, 0, True)
    kinds = []
    for kind in range(2):
        base = kind * half
        parts = (pl.ds(base, half), pl.ds(base, quarter), pl.ds(base + quarter, quarter))
        if kind == 0:
            kinds.append((parts, lambda a, b: moved(a, b)))
        else:
            kinds.append((parts, lambda a, b: moved(b, a)))
    near, across, far, far_across, shared = [], [{}, {}], [[], []], [{}, {}], []

    def open_up():
        for parts, at in kinds:
            near.append([box.push(own.at[parts[0]], out.at[me, parts[0]], dp=at(s, 0)) for s in (1, -1)])
        for k, (parts, at) in enumerate(kinds):
            across[k][0] = [box.push(own.at[parts[0]], out.at[me, parts[0]], dp=at(0, s)) for s in (1, -1)]
        shared.append(box.push(own, out.at[me], dp=sibling))

    def pass_on(k, slot):
        parts, at = kinds[k]
        block = out.at[slot, parts[0]]
        return [box.push(block, block, dp=at(0, t)) for t in (1, -1)]

    def to_sibling(k, slot):
        block = out.at[slot, kinds[k][0][0]]
        shared.append(box.push(block, block, dp=sibling))

    def from_near(i, s):
        def step():
            for k, (parts, at) in enumerate(kinds):
                near[k][i].wait_recv()
                block = out.at[at(s, 0), parts[1 + i]]
                far[k].append(box.push(block, block, dp=at(-s, 0)))
            for k, (parts, at) in enumerate(kinds):
                across[k][s] = pass_on(k, at(s, 0))
                to_sibling(k, at(s, 0))

        return step

    def from_far(k):
        def step():
            for copy in far[k]:
                copy.wait_recv()
            slot = kinds[k][1](2, 0)
            across[k][2] = pass_on(k, slot)
            to_sibling(k, slot)

        return step

    def from_across(k, f):
        def step():
            parts, at = kinds[k]
            far_across[k][f] = []
            for i, s in enumerate((-1, 1)):
                across[k][f][i].wait_recv()
                slot = at(f, s)
                block = out.at[slot, parts[1 + i]]
                far_across[k][f].append(box.push(block, block, dp=at(0, -s)))
                to_sibling(k, slot)

        return step

    def from_far_across(k, f):
        def step():
            for copy in far_across[k][f]:
                copy.wait_recv()
            to_sibling(k, kinds[k][1](f, 2))

        return step

    def close():
        for copy in shared:
            copy.wait_recv()

    steps = [open_up, from_near(0, -1), from_near(1, 1), from_far(0), from_far(1)]
    steps += [from_across(k, f) for f in (0, -1, 1, 2) for k in range(2)]
    steps += [from_far_across(k, f) for f in (0, -1, 1, 2) for k in range(2)]
    return steps + [close]


def gather_peers():
    return [moved(1, 0), moved(-1, 0), moved(0, 1), moved(0, -1), moved(0, 0, True)]


GATHER_COPIES = 71


def half_dot(left, right, dims=(((1,), (0,)), ((), ()))):
    high = right.astype(NARROW)
    low = (right - high.astype(WIDE)).astype(NARROW)
    return lax.dot_general(left, high, dims, preferred_element_type=WIDE) + lax.dot_general(
        left, low, dims, preferred_element_type=WIDE
    )


TURNED = (((0,), (0,)), ((), ()))


def two_parts(value):
    high = value.astype(NARROW)
    return high, (value - high.astype(WIDE)).astype(NARROW)


def wide_dot(left, right, left_dim=1, right_dim=0):
    left_high, left_low = two_parts(left)
    right_high, right_low = two_parts(right)

    def part(one, two):
        return lax.dot_general(one, two, (((left_dim,), (right_dim,)), ((), ())), preferred_element_type=WIDE)

    return part(left_high, right_high) + (part(left_high, right_low) + part(left_low, right_high))


def convolve(pre_ref, taps_ref, part, head, inner, aux):
    count = aux.shape[0]
    cols = slice(part * inner + head * DH, part * inner + (head + 1) * DH)
    taps = taps_ref[:, head * DH : (head + 1) * DH]
    total = pre_ref[pl.ds(HALO, count), cols] * taps[part : part + 1]
    for j in range(1, KW):
        shifted = pre_ref[pl.ds(HALO - j, count), cols]
        total = total + shifted * aux[:, j : j + 1] * taps[3 * j + part : 3 * j + part + 1]
    return total


def masks(aux, seg_row):
    same = aux[:, 6:7] == seg_row
    shape = (aux.shape[0], aux.shape[0])
    row = lax.broadcasted_iota(jnp.int32, shape, 0)
    col = lax.broadcasted_iota(jnp.int32, shape, 1)
    return row, col, same


def each(step, *lists):
    return [step(*items) for items in zip(*lists)]


def lower_inverses(lowers, row, col, tick):
    near = [jnp.where(row // 8 == col // 8, lower, 0.0) for lower in lowers]
    square = each(lambda a: wide_dot(a, a), near)
    inverse = [jnp.where(row == col, 1.0, 0.0) - a for a in near]
    inverse = each(lambda x, s: x + wide_dot(x, s), inverse, square)
    square = each(lambda s: wide_dot(s, s), square)
    inverse = each(lambda x, s: x + wide_dot(x, s), inverse, square)
    size = 8
    while size < row.shape[0]:
        link = (row // (2 * size) == col // (2 * size)) & (row // size != col // size)
        middle = each(lambda lower, x: wide_dot(jnp.where(link, lower, 0.0), x), lowers, inverse)
        inverse = each(lambda x, y: x - wide_dot(x, y), inverse, middle)
        size *= 2
        tick()
    return inverse


def mixer_forward(heads, pre_ref, taps_ref, aux, seg_row, out_ref, reach_ref, map_ref, offset_ref, kept, tick):
    q_ref, k_ref, v_ref, t_ref, w_ref, u_ref = kept
    count = aux.shape[0]
    inner = out_ref.shape[1]
    linked, ending = aux[:, 4:5], aux[:, 5:6]
    row, col, same = masks(aux, seg_row)
    rate = [aux[:, 8 + h : 9 + h] for h in heads]
    cols = [slice(h * DH, (h + 1) * DH) for h in heads]

    def act(part):
        convs = [convolve(pre_ref, taps_ref, part, h, inner, aux) for h in heads]
        return [conv * jax.nn.sigmoid(conv) for conv in convs]

    def unit(a):
        return a * lax.rsqrt(jnp.sum(a * a, axis=1, keepdims=True) + EPSILON)

    k = each(unit, act(1))
    gram = each(lambda b: wide_dot(b, b, 1, 1), k)
    lowers = each(lambda g, r: jnp.where((row > col) & same, g * r, 0.0), gram, rate)
    q, v = each(unit, act(0)), act(2)
    for i in range(len(heads)):
        q_ref[:, cols[i]] = q[i]
        k_ref[:, cols[i]] = k[i]
        v_ref[:, cols[i]] = v[i]
    scores = each(lambda a, b: jnp.where((row >= col) & same, wide_dot(a, b, 1, 1), 0.0), q, k)
    tick()
    inverse = lower_inverses(lowers, row, col, tick)
    written = each(
        lambda t, a, b, r: wide_dot(t, jnp.concatenate([a, b * linked], axis=1) * r), inverse, v, k, rate
    )
    ends = each(lambda b, w: wide_dot(b * ending, w, 0, 0), k, written)
    mixed = each(wide_dot, scores, written)
    eye = jnp.where(row[:DH, :DH] == col[:DH, :DH], 1.0, 0.0)
    last = aux[count - 1 :, 4:5]
    for i, h in enumerate(heads):
        t_ref[h] = inverse[i]
        w_ref[:, cols[i]] = written[i][:, :DH]
        u_ref[:, cols[i]] = written[i][:, DH:]
        offset_ref[h] = ends[i][:, :DH].astype(offset_ref.dtype)
        map_ref[h] = (eye * last - ends[i][:, DH:]).astype(map_ref.dtype)
        out_ref[:, cols[i]] = mixed[i][:, :DH]
        reach_ref[:, cols[i]] = q[i] * linked - mixed[i][:, DH:]
    tick()


def mixer_backward(heads, pre_ref, taps_ref, aux, seg_row, kept, state_ref, grad_ref, d_out_ref, d_ext):
    q_ref, k_ref, v_ref, t_ref, w_ref, u_ref = kept
    count = aux.shape[0]
    inner = d_out_ref.shape[1]
    linked, ending = aux[:, 4:5], aux[:, 5:6]
    row, col, same = masks(aux, seg_row)
    upto = (row >= col) & same
    below = (row > col) & same

    def take(ref):
        return [ref[:, h * DH : (h + 1) * DH] for h in heads]

    rate = [aux[:, 8 + h : 9 + h] for h in heads]
    q, k, v, d_out = take(q_ref), take(k_ref), take(v_ref), take(d_out_ref)
    state, grad = [state_ref[h] for h in heads], [grad_ref[h] for h in heads]
    written = each(lambda w, u, s: w - wide_dot(u, s), take(w_ref), take(u_ref), state)
    scores = each(lambda a, b: jnp.where(upto, wide_dot(a, b, 1, 1), 0.0), q, k)
    d_written = each(
        lambda a, d, b, g: wide_dot(a, d, 0, 0) + wide_dot(b * ending, g), scores, d_out, k, grad
    )
    d_right = each(lambda t, d: wide_dot(t, d, 0, 0), [t_ref[h] for h in heads], d_written)
    d_scores = each(lambda d, w: jnp.where(upto, wide_dot(d, w, 1, 1), 0.0), d_out, written)
    d_lower = each(lambda d, w: jnp.where(below, -wide_dot(d, w, 1, 1), 0.0), d_right, written)
    d_q = each(
        lambda ds, b, d, s: wide_dot(ds, b) + linked * wide_dot(d, s, 1, 1), d_scores, k, d_out, state
    )
    d_k = each(
        lambda ds, a, w, g: wide_dot(ds, a, 0, 0) + ending * wide_dot(w, g, 1, 1), d_scores, q, written, grad
    )
    d_rate = each(
        lambda d, a, b, s: jnp.sum(d * (a - linked * wide_dot(b, s)), axis=1, keepdims=True), d_right, v, k, state
    )
    d_rate = each(
        lambda r, d, b: r + jnp.sum(d * wide_dot(b, b, 1, 1), axis=1, keepdims=True), d_rate, d_lower, k
    )
    d_k = each(lambda dk, r, d, s: dk - (linked * r) * wide_dot(d, s, 1, 1), d_k, rate, d_right, state)
    d_gram = each(lambda d, r: d * r, d_lower, rate)
    d_k = each(lambda dk, d, b: dk + wide_dot(d, b) + wide_dot(d, b, 0, 0), d_k, d_gram, k)
    d_v = each(lambda r, d: r * d, rate, d_right)
    for i, h in enumerate(heads):
        for part, (unit, d) in enumerate(((q[i], d_q[i]), (k[i], d_k[i]), (None, d_v[i]))):
            cols = slice(h * DH, (h + 1) * DH)
            conv = convolve(pre_ref, taps_ref, part, h, inner, aux)
            gate = jax.nn.sigmoid(conv)
            if unit is not None:
                act = conv * gate
                scale = lax.rsqrt(jnp.sum(act * act, axis=1, keepdims=True) + EPSILON)
                d = (d - unit * jnp.sum(unit * d, axis=1, keepdims=True)) * scale
            d_conv = d * gate * (1.0 + conv * (1.0 - gate))
            d_ext[part, :HALO, cols] = jnp.zeros((HALO, DH), WIDE)
            d_ext[part, HALO:, cols] = d_conv * taps_ref[part : part + 1, cols]
            for j in range(1, KW):
                term = d_conv * taps_ref[3 * j + part : 3 * j + part + 1, cols] * aux[:, j : j + 1]
                d_ext[part, pl.ds(HALO - j, count), cols] += term
    return each(lambda d, r: d * r * (1.0 - r), d_rate, rate)


def inverse_rms(values):
    return lax.rsqrt(jnp.mean(values * values, axis=-1, keepdims=True) + EPSILON)


def norm_back(values, scale, gain, grad_out):
    weighted = grad_out * gain
    return scale * weighted - values * scale**3 * jnp.mean(weighted * values, axis=-1, keepdims=True)


def dot(left, right):
    return jnp.dot(left, right, preferred_element_type=WIDE)


def dot_nt(left, right):
    return lax.dot_general(left, right, (((1,), (1,)), ((), ())), preferred_element_type=WIDE)


def dot_tn(left, right):
    return lax.dot_general(left, right, (((0,), (0,)), ((), ())), preferred_element_type=WIDE)


class Chain:
    def __init__(self, box, a_ref, sib_a, chip_a, row_a):
        self.box, self.a_ref, self.sib_a, self.chip_a, self.row_a = box, a_ref, sib_a, chip_a, row_a
        self.y, self.z, self.c = coords()
        self.first = self.c == 0
        self.sibling = moved(0, 0, True)
        self.z_peers = {k: moved(0, k) for k in (1, 2, 3)}
        self.y_peers = {k: moved(k, 0) for k in (1, 2, 3)}
        self.mine = pl.ds(pl.multiple_of(2 * self.c, 2), 2)
        self.theirs = pl.ds(pl.multiple_of(2 * (1 - self.c), 2), 2)

    def peers(self):
        return [self.sibling] + list(self.z_peers.values()) + list(self.y_peers.values())

    def swap(self, ref, sib):
        return self.box.push(ref.at[self.theirs], sib, dp=self.sibling)

    def ordered(self, ref, sib, h):
        own, other = ref[2 * self.c + h], sib[h]
        return jnp.where(self.first, own, other), jnp.where(self.first, other, own)

    def spread(self, refs, place, peers):
        return [self.box.push(ref.at[place], ref.at[place], dp=peers[k]) for k in (2, 1, 3) for ref in refs]

    def start_forward(self, b_ref, sib_b, chip_b, row_b, pass_on):
        self.b_ref, self.sib_b, self.chip_b, self.row_b, self.pass_on = b_ref, sib_b, chip_b, row_b, pass_on
        self.pair = [self.swap(self.a_ref, self.sib_a), self.swap(b_ref, sib_b)]

    def chips_forward(self):
        for copy in self.pair:
            copy.wait_recv()
        self.lower = []
        for h in range(2):
            a_low, a_high = self.ordered(self.a_ref, self.sib_a, h)
            b_low, b_high = self.ordered(self.b_ref, self.sib_b, h)
            self.lower.append((a_low, b_low))
            self.chip_a[self.z, h] = lax.dot(a_high, a_low, preferred_element_type=WIDE).astype(NARROW)
            self.chip_b[self.z, h] = (
                lax.dot(a_high, b_low, preferred_element_type=WIDE) + b_high.astype(WIDE)
            ).astype(NARROW)
        self.ring = self.spread((self.chip_a, self.chip_b), self.z, self.z_peers)

    def rows_forward(self):
        for copy in self.ring:
            copy.wait_recv()
        for h in range(2):
            total_a, total_b = self.chip_a[0, h].astype(WIDE), self.chip_b[0, h].astype(WIDE)
            for i in range(1, 4):
                total_a = half_dot(self.chip_a[i, h], total_a)
                total_b = half_dot(self.chip_a[i, h], total_b) + self.chip_b[i, h].astype(WIDE)
            self.row_a[self.y, h] = total_a.astype(NARROW)
            self.row_b[self.y, h] = total_b.astype(NARROW)
        self.ring = self.spread((self.row_a, self.row_b), self.y, self.y_peers)

    def finish_forward(self, out):
        for copy in self.ring:
            copy.wait_recv()
        for h in range(2):
            state = jnp.zeros((DH, DH), WIDE)
            for i in range(3):
                longer = half_dot(self.row_a[i, h], state) + self.row_b[i, h].astype(WIDE)
                state = jnp.where(i < self.y, longer, state)
            for i in range(3):
                longer = half_dot(self.chip_a[i, h], state) + self.chip_b[i, h].astype(WIDE)
                state = jnp.where(i < self.z, longer, state)
            a_low, b_low = self.lower[h]
            middle = half_dot(a_low, state) + b_low.astype(WIDE)
            out[2 * self.c + h] = jnp.where(self.first, state, middle)
            self.pass_on[h] = jnp.where(self.first, middle, state)
        self.box.push(self.pass_on, out.at[self.mine], dp=self.sibling).wait_recv()

    def start_backward(self, g_ref, sib_g, chip_g, row_g, pass_on):
        self.g_ref, self.sib_g, self.chip_g, self.row_g, self.pass_on = g_ref, sib_g, chip_g, row_g, pass_on
        self.pair = [self.swap(g_ref, sib_g)]

    def chips_backward(self):
        for copy in self.pair:
            copy.wait_recv()
        self.upper_g = []
        for h in range(2):
            a_low, _ = self.ordered(self.a_ref, self.sib_a, h)
            g_low, g_high = self.ordered(self.g_ref, self.sib_g, h)
            self.upper_g.append(g_high)
            self.chip_g[self.z, h] = (
                lax.dot_general(a_low, g_high, TURNED, preferred_element_type=WIDE) + g_low.astype(WIDE)
            ).astype(NARROW)
        self.ring = self.spread((self.chip_g,), self.z, self.z_peers)

    def rows_backward(self):
        for copy in self.ring:
            copy.wait_recv()
        for h in range(2):
            total = self.chip_g[3, h].astype(WIDE)
            for i in (2, 1, 0):
                total = half_dot(self.chip_a[i, h], total, TURNED) + self.chip_g[i, h].astype(WIDE)
            self.row_g[self.y, h] = total.astype(NARROW)
        self.ring = self.spread((self.row_g,), self.y, self.y_peers)

    def finish_backward(self, out):
        for copy in self.ring:
            copy.wait_recv()
        for h in range(2):
            grad = jnp.zeros((DH, DH), WIDE)
            for i in (3, 2, 1):
                longer = half_dot(self.row_a[i, h], grad, TURNED) + self.row_g[i, h].astype(WIDE)
                grad = jnp.where(i > self.y, longer, grad)
            for i in (3, 2, 1):
                longer = half_dot(self.chip_a[i, h], grad, TURNED) + self.chip_g[i, h].astype(WIDE)
                grad = jnp.where(i > self.z, longer, grad)
            _, a_high = self.ordered(self.a_ref, self.sib_a, h)
            middle = half_dot(a_high, grad, TURNED) + self.upper_g[h].astype(WIDE)
            out[2 * self.c + h] = jnp.where(self.first, middle, grad)
            self.pass_on[h] = jnp.where(self.first, grad, middle)
        self.box.push(self.pass_on, out.at[self.mine], dp=self.sibling).wait_recv()


def columns(i, width):
    return pl.ds(pl.multiple_of(i * width, width), width)


class MpSum:
    ORDER = (2, 1, 3)

    def __init__(self, box, part, landed):
        self.box, self.part, self.landed = box, part, landed
        self.m = lax.axis_index("mp")
        self.peers = {k: lax.rem(self.m + k, 4) for k in (1, 2, 3)}
        self.copies = []

    def owner(self, k):
        return lax.rem(self.m + k, 4)

    def send(self, k):
        self.copies.append(self.box.push(self.part.at[k], self.landed.at[k - 1], mp=self.peers[k]))

    def total(self):
        for copy in self.copies:
            copy.wait_recv()
        total = self.part[0].astype(WIDE)
        for k in range(3):
            total = total + self.landed[k].astype(WIDE)
        return total

    def share(self, out, width):
        block = out.at[:, columns(self.m, width)]
        return [self.box.push(block, block, mp=self.peers[k]) for k in self.ORDER]


def unpack_ranks(block, spread, ranks, first, tiles):
    for q in range(4):
        for t in range(tiles):
            at = first + q * tiles + t
            spread[t, pl.ds(q, 32, stride=4), :] = block[at // 64, pl.ds(at % 64, 32, stride=64), :]
    for t in range(tiles):
        ranks[:, t * 128 : (t + 1) * 128] = spread[t].astype(ranks.dtype)


def front_kernel(
    x_ref, g_own, seg_ref, adapters, norm_ref, gain_ref, bias_ref, taps_ref, wide_ref, thin_ref, late_ref, late_thin,
    wide_out, thin_out, late_out, pre, aux_ref, picks_ref, xn_ref, u_ref, q_ref, k_ref, v_ref, t_ref, w_ref, u_map_ref,
    reach, ranks, a_ref, sib_a, chip_a, row_a, state_out, mixer_out, normed, u_out_ref, branch, g_full,
    wide_all, thin_all, late_all, thin_own, late_own, halo_x, seg_ext, xn_ext, pre_wide, block, spread, b_beta,
    b_ref, out_zero, sib_b, chip_b, row_b, pass_on, part, landed, send, recv, local,
):
    count, model = x_ref.shape
    heads = a_ref.shape[0]
    inner = heads * DH
    m = lax.axis_index("mp")
    place = lax.axis_index("dp")
    before, after = lax.rem(place + 31, 32), lax.rem(place + 1, 32)
    mp_peers = {k: lax.rem(m + k, 4) for k in (1, 2, 3)}
    box = Mailbox(send, recv)
    chain = Chain(box, a_ref, sib_a, chip_a, row_a)
    greet([before, after] + chain.peers(), list(mp_peers.values()))
    me = moved(0, 0)
    seg_ext[HALO:] = jnp.concatenate([seg_ref[...]] * 16, axis=0).T
    edges = [
        box.push(x_ref.at[pl.ds(count - HALO, HALO)], halo_x, dp=after),
        box.push(seg_ext.at[pl.ds(count, HALO)], seg_ext.at[pl.ds(0, HALO)], dp=after),
    ]
    thin_rows = thin_ref.shape[0]
    mine = pl.ds(pl.multiple_of(m * thin_rows, thin_rows), thin_rows)
    crossing = [box.push(thin_ref, thin_own.at[mine], mp=peer) for peer in mp_peers.values()]
    late_cols = pl.ds(late_ref.shape[1], late_thin.shape[1])
    late_crossing = [box.push(late_thin, late_own.at[mine, late_cols], mp=peer) for peer in mp_peers.values()]
    keep = [
        pltpu.make_async_copy(wide_ref, wide_all.at[me], local.at[0]),
        pltpu.make_async_copy(thin_ref, thin_own.at[mine], local.at[1]),
        pltpu.make_async_copy(late_ref, late_own.at[:, pl.ds(0, late_ref.shape[1])], local.at[2]),
        pltpu.make_async_copy(late_thin, late_own.at[mine, late_cols], local.at[3]),
    ]
    for copy in keep:
        copy.start()
    wide_steps = gather_steps(box, wide_ref, wide_all)
    thin_steps = gather_steps(box, thin_own, thin_all)
    late_steps = gather_steps(box, late_own, late_all)
    wide_steps.pop(0)()
    share = g_own.shape[1]
    g_full[:, columns(m, share)] = g_own[...]
    keep[1].wait()
    for copy in crossing:
        copy.wait_recv()
    keep_thin = pltpu.make_async_copy(thin_own, thin_all.at[me], local.at[4])
    keep_thin.start()
    thin_steps.pop(0)()
    g_sent = [box.push(g_own, g_full.at[:, columns(m, share)], mp=mp_peers[k]) for k in MpSum.ORDER]

    def normal(rows):
        rows = rows.astype(WIDE)
        return (rows * inverse_rms(rows) * norm_ref[0:1, :]).astype(NARROW)

    xn_ref[...] = normal(x_ref[...])
    xn_ext[HALO:] = xn_ref[...]
    for one, two in zip(wide_steps, thin_steps):
        one()
        two()
    keep[0].wait()
    keep_thin.wait()
    keep[2].wait()
    keep[3].wait()
    for copy in late_crossing:
        copy.wait_recv()
    keep_late = pltpu.make_async_copy(late_own, late_all.at[me], local.at[5])
    keep_late.start()
    late_steps.pop(0)()
    to_hbm = [
        pltpu.make_async_copy(wide_all, wide_out, local.at[6]),
        pltpu.make_async_copy(thin_all, thin_out, local.at[7]),
    ]
    for copy in to_hbm:
        copy.start()

    def tick(steps=1):
        for _ in range(min(steps, len(late_steps))):
            late_steps.pop(0)()

    for copy in edges:
        copy.wait_recv()
    xn_ext[:HALO] = normal(halo_x[...])
    seg_ext[:HALO] = jnp.where(place == 0, -1.0, seg_ext[:HALO])
    lanes = lax.broadcasted_iota(jnp.int32, seg_ext.shape, 1)
    seg_all = seg_ext[...]
    per_token = jnp.zeros(seg_all.shape, WIDE)
    for s in range(adapters.shape[0]):
        per_token = jnp.where(seg_all == float(s), adapters[s].astype(WIDE), per_token)
    picks_ext = jnp.where(per_token == (lanes // RANK).astype(WIDE), 1.0, 0.0)
    picks_ref[...] = picks_ext[HALO:]
    tiles = inner // 128
    for i in range(2):
        lane_block = slice(3 * inner + i * 128, 3 * inner + (i + 1) * 128)
        block[i] = wide_all[:, :, lane_block].reshape(model, 128).astype(WIDE)
    for q in range(4):
        b_beta[pl.ds(q, 32, stride=4), :] = block[0, pl.ds(q, 32, stride=64), :]
    unpack_ranks(block.at[pl.ds(1, 1)], spread, ranks.at[:, pl.ds(0, 4 * inner)], 0, 4 * tiles)
    beta = pltpu.roll(b_beta[...], 64, 1)
    beta_lane = lax.broadcasted_iota(jnp.int32, beta.shape, 1)
    beta = jnp.where((beta_lane >= 8) & (beta_lane < 8 + heads), beta, 0.0)
    ranks[:, 4 * inner :] = beta.astype(NARROW)
    tick()
    u_ext = dot(xn_ext[...], thin_all[...].reshape(model, thin_all.shape[2]))
    u_ext = (u_ext * jnp.concatenate([picks_ext] * 4, axis=1)).astype(NARROW)
    u_ref[...] = u_ext[HALO:]
    tick()
    for j in range(3):
        cols = slice(j * inner, (j + 1) * inner)
        value = dot(xn_ext[...], wide_all[:, :, cols].reshape(model, inner)) + dot(
            u_ext[:, j * 128 : (j + 1) * 128], ranks[:, cols]
        )
        value = value.astype(NARROW)
        pre[:, cols] = value
        pre_wide[:, cols] = value.astype(WIDE)
        tick()
    w_beta = wide_all[:, :, 3 * inner : 3 * inner + 128].reshape(model, 128)
    logits = dot(xn_ref[...], w_beta) + dot(u_ref[:, 384:], ranks[:, 4 * inner :]) + bias_ref[0:1, :]
    seg = seg_all[HALO:]
    lane = lanes[HALO:]
    aux = jnp.where((lane >= 8) & (lane < 8 + heads), jax.nn.sigmoid(logits), 0.0)
    for j in range(KW):
        aux = jnp.where((lane == j) & (seg_ext[pl.ds(HALO - j, count)] == seg), 1.0, aux)
    aux = jnp.where((lane == 4) & (seg == seg_ext[HALO - 1 : HALO]), 1.0, aux)
    aux = jnp.where((lane == 5) & (seg == seg_ext[HALO + count - 1 : HALO + count]), 1.0, aux)
    aux = jnp.where(lane == 6, seg, aux)
    aux_ref[...] = aux
    for first in range(0, heads, 2):
        mixer_forward(
            list(range(first, min(first + 2, heads))), pre_wide, taps_ref, aux, seg_ref[0:1, :],
            out_zero, reach, a_ref, b_ref, (q_ref, k_ref, v_ref, t_ref, w_ref, u_map_ref), tick,
        )
    chain.start_forward(b_ref, sib_b, chip_b, row_b, pass_on)
    tick(len(late_steps))
    keep_late.wait()
    keep_late_out = pltpu.make_async_copy(late_all, late_out, local.at[8])
    keep_late_out.start()
    chain.chips_forward()
    chain.rows_forward()
    chain.finish_forward(state_out)
    for h in range(heads):
        cols = slice(h * DH, (h + 1) * DH)
        rows = out_zero[:, cols] + wide_dot(reach[:, cols], state_out[h])
        mixer_out[:, cols] = rows
        normed[:, cols] = (rows * inverse_rms(rows) * gain_ref[0:1, :]).astype(NARROW)
    u_out = (dot_nt(normed[...], ranks[:, 3 * inner : 4 * inner]) * picks_ref[...]).astype(NARROW)
    u_out_ref[...] = u_out
    one = MpSum(box, part, landed)
    for k in (2, 1, 3, 0):
        groups = pl.ds(one.owner(k) * (share // 64), share // 64)
        w_out = late_all[groups, :, :inner].reshape(share, inner)
        b_mix = late_all[groups, :, inner + 256 : inner + 384].reshape(share, 128)
        part[k] = (dot_nt(normed[...], w_out) + dot_nt(u_out, b_mix)).astype(NARROW)
        if k:
            one.send(k)
    branch[:, columns(m, share)] = one.total().astype(NARROW)
    for copy in g_sent + one.share(branch, share):
        copy.wait_recv()
    for copy in to_hbm + [keep_late_out]:
        copy.wait()
    box.drain()


def front(x, g, seg_row, adapters, norm, gain, bias, taps, wide, thin, late, late_thin):
    count, model = x.shape
    inner = taps.shape[1]
    heads = inner // DH
    share = g.shape[1]
    vmem = pl.BlockSpec(memory_space=pltpu.VMEM)
    anywhere = pl.BlockSpec(memory_space=pl.ANY)
    two = (2, DH, DH)
    square = (heads, DH, DH)
    by_head = ((count, inner), WIDE)
    thin_all, late_all = (32, 64, thin.shape[1]), (32, 64, late.shape[1] + late_thin.shape[1])
    results = [
        ((32,) + wide.shape, NARROW),
        (thin_all, NARROW),
        (late_all, NARROW),
        ((HALO + count, 3 * inner), NARROW),
        ((count, 128), WIDE),
        ((count, 128), WIDE),
        ((count, model), NARROW),
        ((count, 512), NARROW),
        by_head,
        by_head,
        by_head,
        ((heads, count, count), WIDE),
        by_head,
        by_head,
        by_head,
        ((128, 4 * inner + 128), NARROW),
        (square, NARROW),
        (two, NARROW),
        ((4,) + two, NARROW),
        ((4,) + two, NARROW),
        (square, WIDE),
        by_head,
        ((count, inner), NARROW),
        ((count, 128), NARROW),
        ((count, model), NARROW),
        ((count, model), NARROW),
    ]
    scratch = [
        ((32,) + wide.shape, NARROW),
        (thin_all, NARROW),
        (late_all, NARROW),
        (thin_all[1:], NARROW),
        (late_all[1:], NARROW),
        ((HALO, model), NARROW),
        ((HALO + count, 128), WIDE),
        ((HALO + count, model), NARROW),
        ((HALO + count, 3 * inner), WIDE),
        ((2, model, 128), WIDE),
        ((4 * inner // 128, 128, 128), WIDE),
        ((128, 128), WIDE),
        (square, NARROW),
        by_head,
        (two, NARROW),
        ((4,) + two, NARROW),
        ((4,) + two, NARROW),
        (two, WIDE),
        ((4, count, share), NARROW),
        ((3, count, share), NARROW),
    ]
    copies = 3 * GATHER_COPIES + 2 + 3 + 3 + 3 + 2 + 6 + 6 + 1 + 6
    return pl.pallas_call(
        front_kernel,
        out_shape=tuple(jax.ShapeDtypeStruct(*r) for r in results),
        in_specs=[vmem] * 3 + [pl.BlockSpec(memory_space=pltpu.SMEM)] + [vmem] * 4 + [anywhere] * 4,
        out_specs=tuple([anywhere] * 3 + [vmem] * (len(results) - 3)),
        scratch_shapes=[pltpu.VMEM(*s) for s in scratch]
        + [
            pltpu.SemaphoreType.DMA((copies,)),
            pltpu.SemaphoreType.DMA((copies,)),
            pltpu.SemaphoreType.DMA((9,)),
        ],
        compiler_params=pltpu.CompilerParams(
            collective_id=0, has_side_effects=True, vmem_limit_bytes=60 << 20
        ),
        name="front",
    )(x, g, seg_row, adapters, norm, gain, bias, taps, wide, thin, late, late_thin)


def middle_kernel(
    a_ref, sib_a, chip_a, row_a, reach, mixer_out, normed, u_out_ref, branch, picks_ref, x_ref, g_full, norm_ref, gain_ref,
    ranks_one, late_ref, wide_ref,
    output, grad_out, d_one_out, d_mixer_out, g_b_ffn, g_a_down, g_a_out, g_shared,
    late, w_gu, w_down, packed, block, spread, ranks, sib_g, chip_g, row_g, pass_on, g_maps,
    part, landed, hidden_one, xn_two, gate, up, hidden, ffn_part, ffn_landed,
    d_gate_up, d_xn, extra, extra_landed, d_branch, e_down_ref, u_two_ref,
    send, recv, local,
):
    count = x_ref.shape[0]
    heads = a_ref.shape[0]
    inner = heads * DH
    ff = gate.shape[1]
    model = x_ref.shape[1]
    share = output.shape[1]
    m = lax.axis_index("mp")
    loads = [
        pltpu.make_async_copy(late_ref, late, local.at[0]),
        pltpu.make_async_copy(wide_ref.at[:, pl.ds(3 * ff, packed.shape[1])], packed, local.at[1]),
        pltpu.make_async_copy(wide_ref.at[:, pl.ds(0, ff)], w_gu.at[:, pl.ds(0, ff)], local.at[2]),
        pltpu.make_async_copy(wide_ref.at[:, pl.ds(ff, ff)], w_gu.at[:, pl.ds(ff, ff)], local.at[3]),
        pltpu.make_async_copy(wide_ref.at[:, pl.ds(2 * ff, ff)], w_down, local.at[4]),
    ]
    for load in loads:
        load.start()
    box = Mailbox(send, recv)
    chain = Chain(box, a_ref, sib_a, chip_a, row_a)
    mp_peers = {k: lax.rem(m + k, 4) for k in (1, 2, 3)}
    greet(chain.peers(), list(mp_peers.values()))
    picks = picks_ref[...]
    u_out = u_out_ref[...]
    a_out = ranks_one.at[:, pl.ds(3 * inner, inner)]
    a_down = ranks.at[:, pl.ds(2 * ff, ff)]
    w_out, a_two = late.at[:, pl.ds(0, inner)], late.at[:, pl.ds(inner, 256)]
    b_mix, b_down = late.at[:, pl.ds(inner + 256, 128)], late.at[:, pl.ds(inner + 384, 128)]

    rows = x_ref[...].astype(WIDE) + branch[...].astype(WIDE)
    hidden_one[...] = rows
    scale_two = inverse_rms(rows)
    xn_two[...] = (rows * scale_two * norm_ref[0:1, :]).astype(NARROW)
    two_picks = jnp.concatenate([picks, picks], axis=1)
    loads[0].wait()
    u_two_ref[...] = (dot(xn_two[...], a_two[...]) * two_picks).astype(NARROW)
    loads[1].wait()
    for i in range(3):
        block[i] = packed[:, i * 128 : (i + 1) * 128].astype(WIDE)
    unpack_ranks(block, spread, ranks, 0, 3 * ff // 128)
    loads[2].wait()
    gate[...] = dot(xn_two[...], w_gu[:, :ff]) + dot(u_two_ref[:, :128], ranks[:, :ff])
    loads[3].wait()
    up[...] = dot(xn_two[...], w_gu[:, ff:]) + dot(u_two_ref[:, 128:], ranks[:, ff : 2 * ff])
    hidden[...] = (gate[...] * jax.nn.sigmoid(gate[...]) * up[...]).astype(NARROW)
    loads[4].wait()

    e_down = (dot(g_full[...], b_down[...]) * picks).astype(NARROW)
    e_down_ref[...] = e_down
    d_hidden = dot(g_full[...], w_down[...]) + dot(e_down, a_down[...])
    sig = jax.nn.sigmoid(gate[...])
    d_gate_up[:, :ff] = (d_hidden * up[...] * sig * (1.0 + gate[...] * (1.0 - sig))).astype(NARROW)
    d_gate_up[:, ff:] = (d_hidden * gate[...] * sig).astype(NARROW)
    e_two = [
        (dot_nt(d_gate_up[:, j * ff : (j + 1) * ff], ranks[:, j * ff : (j + 1) * ff]) * picks).astype(NARROW)
        for j in range(2)
    ]
    two = MpSum(box, part, landed)
    for k in (2, 1, 3, 0):
        rows = columns(two.owner(k), share)
        part[k] = (
            dot_nt(d_gate_up[...], w_gu[rows, :]) + dot_nt(jnp.concatenate(e_two, axis=1), a_two[rows, :])
        ).astype(NARROW)
        if k:
            two.send(k)
    u_down = (dot_nt(hidden[...], a_down[...]) * picks).astype(NARROW)
    for j, value in enumerate((e_two[0], e_two[1], u_out, u_down)):
        extra[j] = value
    d_xn[:, columns(m, share)] = two.total().astype(NARROW)
    shared = two.share(d_xn, share)
    extra_sent = [box.push(extra.at[mp_peers[k]], extra_landed.at[k - 1], mp=mp_peers[k]) for k in MpSum.ORDER]
    three = MpSum(box, ffn_part, ffn_landed)
    for k in (2, 1, 3, 0):
        rows = columns(three.owner(k), share)
        ffn_part[k] = (dot_nt(hidden[...], w_down[rows, :]) + dot_nt(u_down, b_down[rows, :])).astype(NARROW)
    for copy in shared:
        copy.wait_recv()
    for k in MpSum.ORDER:
        three.send(k)

    rows = hidden_one[...]
    scale_two = inverse_rms(rows)
    d_one = g_full[...].astype(WIDE) + norm_back(rows, scale_two, norm_ref[0:1, :], d_xn[...].astype(WIDE))
    d_one_out[...] = d_one
    d_branch[...] = d_one.astype(NARROW)
    e_out = (dot(d_branch[...], b_mix[...]) * picks).astype(NARROW)
    d_normed = dot(d_branch[...], w_out[...]) + dot(e_out, a_out[...])
    for h in range(heads):
        cols = slice(h * DH, (h + 1) * DH)
        rows = mixer_out[:, cols]
        d_rows = norm_back(rows, inverse_rms(rows), gain_ref[0:1, :], d_normed[:, cols])
        d_mixer_out[:, cols] = d_rows
        g_maps[h] = wide_dot(reach[:, cols], d_rows, 0, 0).astype(NARROW)
    chain.start_backward(g_maps, sib_g, chip_g, row_g, pass_on)
    g_a_out[...] = dot_tn(e_out, normed[...]).astype(NARROW)
    chain.chips_backward()
    for j in range(2):
        cols = slice(j * ff, (j + 1) * ff)
        g_b_ffn[:, cols] = dot_tn(u_two_ref[:, j * 128 : (j + 1) * 128], d_gate_up[:, cols]).astype(NARROW)
    chain.rows_backward()
    g_a_down[...] = dot_tn(e_down_ref[...], hidden[...]).astype(NARROW)
    for copy in extra_sent:
        copy.wait_recv()
    factor = extra[m].astype(WIDE)
    for k in range(3):
        factor = factor + extra_landed[k].astype(WIDE)
    left = jnp.where(m < 2, xn_two[...], jnp.where(m == 2, d_branch[...], g_full[...]))
    g_shared[...] = dot_tn(left, factor.astype(NARROW)).astype(NARROW)
    chain.finish_backward(grad_out)
    output[...] = (hidden_one[:, columns(m, share)] + three.total()).astype(NARROW)
    box.drain()


def middle(kept_maps, forward, x, g, norm, gain, ranks, late, wide):
    operands = (*kept_maps, *forward, x, g, norm, gain, ranks)
    count, inner = forward[0].shape
    heads = inner // DH
    model = x.shape[1]
    share = model // 4
    ff = (wide.shape[1] - 384) // 3
    vmem = pl.BlockSpec(memory_space=pltpu.VMEM)
    anywhere = pl.BlockSpec(memory_space=pl.ANY)
    two = (2, DH, DH)
    copies = 1 + 3 + 3 + 1 + 6 + 3 + 3
    results = [
        ((count, share), NARROW),
        ((heads, DH, DH), WIDE),
        ((count, model), WIDE),
        ((count, inner), WIDE),
        ((128, 2 * ff), NARROW),
        ((128, ff), NARROW),
        ((128, inner), NARROW),
        ((model, 128), NARROW),
    ]
    scratch = [
        (late.shape, NARROW),
        ((model, 2 * ff), NARROW),
        ((model, ff), NARROW),
        ((model, 384), NARROW),
        ((3, model, 128), WIDE),
        ((3 * ff // 128, 128, 128), WIDE),
        ((128, 3 * ff), NARROW),
        (two, NARROW),
        ((4,) + two, NARROW),
        ((4,) + two, NARROW),
        (two, WIDE),
        ((heads, DH, DH), NARROW),
        ((4, count, share), NARROW),
        ((3, count, share), NARROW),
        ((count, model), WIDE),
        ((count, model), NARROW),
        ((count, ff), WIDE),
        ((count, ff), WIDE),
        ((count, ff), NARROW),
        ((4, count, share), NARROW),
        ((3, count, share), NARROW),
        ((count, 2 * ff), NARROW),
        ((count, model), NARROW),
        ((4, count, 128), NARROW),
        ((3, count, 128), NARROW),
        ((count, model), NARROW),
        ((count, 128), NARROW),
        ((count, 256), NARROW),
    ]
    return pl.pallas_call(
        middle_kernel,
        out_shape=tuple(jax.ShapeDtypeStruct(*r) for r in results),
        in_specs=[vmem] * len(operands) + [anywhere] * 2,
        out_specs=tuple([vmem] * len(results)),
        scratch_shapes=[pltpu.VMEM(*v) for v in scratch]
        + [
            pltpu.SemaphoreType.DMA((copies,)),
            pltpu.SemaphoreType.DMA((copies,)),
            pltpu.SemaphoreType.DMA((5,)),
        ],
        compiler_params=pltpu.CompilerParams(
            collective_id=2, has_side_effects=True, vmem_limit_bytes=60 << 20
        ),
        name="middle",
    )(*operands, late, wide)


class DpSum:
    SCRATCH = 6

    @staticmethod
    def scratch(rows, width):
        small = rows // 4
        return [
            ((2, 4, rows, width), NARROW),
            ((4, rows, width), NARROW),
            ((3, rows, width), NARROW),
            ((4, small, width), WIDE),
            ((3, small, width), WIDE),
            ((small, width), WIDE),
        ]

    def __init__(self, box, full, landed_core, landed_y, by_z, landed_z, result):
        self.box, self.full, self.landed_core = box, full, landed_core
        self.landed_y, self.by_z, self.landed_z, self.result = landed_y, by_z, landed_z, result
        self.y, self.z, self.c = coords()

    def over_cores(self):
        self.pair = self.box.push(self.full.at[1 - self.c], self.landed_core, dp=moved(0, 0, True))

    def over_y(self):
        self.pair.wait_recv()
        mine = self.full.at[self.c]
        for i in range(4):
            mine[i] = (mine[i].astype(WIDE) + self.landed_core[i].astype(WIDE)).astype(NARROW)
        self.copies = [
            self.box.push(mine.at[lax.rem(self.y + k, 4)], self.landed_y.at[k - 1], dp=moved(k, 0)) for k in (2, 1, 3)
        ]

    def over_z(self):
        for copy in self.copies:
            copy.wait_recv()
        total = self.full[self.c, self.y].astype(WIDE)
        for k in range(3):
            total = total + self.landed_y[k].astype(WIDE)
        self.by_z[...] = total.reshape(self.by_z.shape)
        self.copies = [
            self.box.push(self.by_z.at[lax.rem(self.z + k, 4)], self.landed_z.at[k - 1], dp=moved(0, k))
            for k in (2, 1, 3)
        ]

    def finish(self):
        for copy in self.copies:
            copy.wait_recv()
        total = self.by_z[self.z]
        for k in range(3):
            total = total + self.landed_z[k]
        self.result[...] = total


def tail_kernel(
    pre_ref, taps_ref, aux_ref, seg_ref, q_ref, k_ref, v_ref, t_ref, w_ref, u_map_ref, state_ref, grad_ref, d_out_ref,
    u_ref, xn_ref, x_ref, d_one_ref, norm_ref, picks_ref, ranks, shared_two, g_b_ffn, g_a_out, g_a_down,
    wide_ref, thin_ref,
    grad_input, out_a_in, out_heads, out_beta, out_a_out, out_ffn, out_a_down, out_res,
    w_in, a_one, d_ext, pre_wide, halo, d_pre, e_one, part, landed, extra_landed, sums, sums_landed, pair, early_pair, ends,
    *rest,
):
    one, two, three, four = (rest[i * DpSum.SCRATCH : (i + 1) * DpSum.SCRATCH] for i in range(4))
    send, recv, local = rest[4 * DpSum.SCRATCH :]
    count, model = x_ref.shape
    inner = d_out_ref.shape[1]
    heads = inner // DH
    ff = g_a_down.shape[1]
    m = lax.axis_index("mp")
    c = lax.rem(lax.axis_index("dp"), 2)
    before, after = (lax.rem(lax.axis_index("dp") + k, 32) for k in (31, 1))
    mp_peers = {k: lax.rem(m + k, 4) for k in (1, 2, 3)}
    dp_peers = [before, after, moved(0, 0, True)]
    dp_peers += [moved(k, 0) for k in (1, 2, 3)] + [moved(0, k) for k in (1, 2, 3)]
    greet(dp_peers, list(mp_peers.values()))
    box = Mailbox(send, recv)
    early_sum, heads_sum, two_sum, one_sum = (DpSum(box, *refs) for refs in (four, one, two, three))

    def halves(refs, values):
        half = refs[0].shape[3]
        missing = 2 * half - sum(value.shape[1] for value in values)
        values = values + [jnp.zeros((128, missing), NARROW)] if missing else values
        values = jnp.concatenate(values, axis=1)
        for i in range(2):
            refs[0][i] = values[:, i * half : (i + 1) * half].reshape(4, 32, half)

    def by_core(value):
        value = value.reshape(4, 4, 2, model // 32, 128)
        return [value[:, :, i].reshape(4, model // 8, 128) for i in range(2)]

    halves(four, [g_b_ffn[...], g_a_out[...], g_a_down[...]])
    early_sum.over_cores()
    for i, value in enumerate(by_core(shared_two[...])):
        two[0][i] = value
    two_sum.over_cores()
    loads = [
        pltpu.make_async_copy(wide_ref.at[:, pl.ds(0, w_in.shape[1])], w_in, local.at[0]),
        pltpu.make_async_copy(thin_ref.at[:, pl.ds(0, a_one.shape[1])], a_one, local.at[1]),
    ]
    for load in loads:
        load.start()
    aux = aux_ref[...]
    pre_wide[...] = pre_ref[...].astype(WIDE)
    kept = (q_ref, k_ref, v_ref, t_ref, w_ref, u_map_ref)
    lanes = lax.broadcasted_iota(jnp.int32, aux.shape, 1)
    d_logit = jnp.zeros(aux.shape, WIDE)
    for first in range(0, heads, 2):
        some = list(range(first, min(first + 2, heads)))
        found = mixer_backward(
            some, pre_wide, taps_ref, aux, seg_ref[0:1, :], kept, state_ref, grad_ref, d_out_ref, d_ext
        )
        for h, value in zip(some, found):
            d_logit = jnp.where(lanes == 8 + h, value, d_logit)
        if first == 0:
            early_sum.over_y()
            two_sum.over_y()
    edges = [box.push(d_ext.at[i, pl.ds(HALO - 8, 8)], halo.at[i], dp=before) for i in range(3)]
    early_sum.over_z()
    two_sum.over_z()
    picks = picks_ref[...]
    d_logit = d_logit.astype(NARROW)
    for copy in edges:
        copy.wait_recv()
    for i in range(3):
        ref = d_ext.at[i]
        cols = slice(i * inner, (i + 1) * inner)
        d_pre[: count - 16, cols] = ref[HALO : HALO + count - 16].astype(NARROW)
        ending = ref[HALO + count - 16 :]
        d_pre[count - 16 :, cols] = jnp.concatenate([ending[:8], ending[8:] + halo[i]], axis=0).astype(NARROW)
    for j in range(3):
        cols = slice(j * inner, (j + 1) * inner)
        e_one[j] = (dot_nt(d_pre[:, cols], ranks[:, cols]) * picks).astype(NARROW)
    e_one[3] = (dot_nt(d_logit, ranks[:, 4 * inner :]) * picks).astype(NARROW)
    extra_sent = [box.push(e_one.at[mp_peers[k]], extra_landed.at[k - 1], mp=mp_peers[k]) for k in MpSum.ORDER]
    grads = [dot_tn(u_ref[:, j * 128 : (j + 1) * 128], d_pre[:, j * inner : (j + 1) * inner]) for j in range(3)]
    grads.append(dot_tn(u_ref[:, 384:], d_logit))
    halves(one, [value.astype(NARROW) for value in grads])
    heads_sum.over_cores()
    for load in loads:
        load.wait()
    share = grad_input.shape[1]
    total = MpSum(box, part, landed)
    row_sum = jnp.zeros((count, 128), WIDE)
    all_e = jnp.concatenate([e_one[j] for j in range(4)], axis=1)
    for k in (2, 1, 3, 0):
        owner = total.owner(k)
        rows = columns(owner, share)
        value = (
            dot_nt(d_pre[...], w_in[rows, : 3 * inner])
            + dot_nt(d_logit, w_in[rows, 3 * inner :])
            + dot_nt(all_e, a_one[rows, :])
        )
        part[k] = value.astype(NARROW)
        if k:
            total.send(k)
        weighted = value * norm_ref[0:1, rows] * x_ref[:, rows].astype(WIDE)
        row_sum = row_sum + jnp.sum(weighted, axis=1, keepdims=True)
    sums[...] = row_sum.T[:8]
    sums_sent = [box.push(sums, sums_landed.at[k - 1], mp=mp_peers[k]) for k in MpSum.ORDER]
    heads_sum.over_y()
    early_sum.finish()
    early_pair[c] = four[5][...]
    early_paired = box.push(four[5], early_pair.at[c], dp=moved(0, 0, True))
    for copy in extra_sent:
        copy.wait_recv()
    factor = e_one[m].astype(WIDE)
    for k in range(3):
        factor = factor + extra_landed[k].astype(WIDE)
    for i, value in enumerate(by_core(dot_tn(xn_ref[...], factor.astype(NARROW)).astype(NARROW))):
        three[0][i] = value
    one_sum.over_cores()
    heads_sum.over_z()
    one_sum.over_y()
    x_all = x_ref[...].astype(WIDE)
    scale = inverse_rms(x_all)
    mine = columns(m, share)
    d_xn = total.total()
    for copy in sums_sent:
        copy.wait_recv()
    rows = sums[...] + sums_landed[0] + sums_landed[1] + sums_landed[2]
    mean = jnp.concatenate([rows] * 16, axis=0).T[:, :1] / model
    grad_input[...] = d_one_ref[:, mine] + (
        scale * norm_ref[0:1, mine] * d_xn - x_ref[:, mine].astype(WIDE) * (scale * scale * scale * mean)
    )
    heads_sum.finish()
    pair[c] = one[5][...]
    paired = box.push(one[5], pair.at[c], dp=moved(0, 0, True))
    two_sum.finish()
    rank_rows = model // 128
    one_sum.over_z()

    def to_owners(slot, result):
        ends[slot, m] = result[columns(m, rank_rows)]
        return [
            box.push(result.at[columns(mp_peers[k], rank_rows)], ends.at[slot, m], mp=mp_peers[k])
            for k in MpSum.ORDER
        ]

    owners = to_owners(1, two[5])
    one_sum.finish()
    owners += to_owners(0, three[5])
    paired.wait_recv()
    early_paired.wait_recv()

    def own_ranks(pair):
        both = jnp.concatenate([pair[0], pair[1]], axis=1)
        return jnp.where(c == 0, both[:4], both[4:])

    rows = own_ranks(pair)
    for j in range(3):
        out_heads[j] = rows[:, j * inner : (j + 1) * inner]
    out_beta[...] = rows[:, 3 * inner + 8 : 3 * inner + 8 + heads]
    rows = own_ranks(early_pair)
    for j in range(2):
        out_ffn[j] = rows[:, j * ff : (j + 1) * ff]
    out_a_out[...] = rows[:, 2 * ff : 2 * ff + inner]
    out_a_down[...] = rows[:, 2 * ff + inner : 3 * ff + inner]
    for copy in owners:
        copy.wait_recv()
    for j in range(4):
        out_a_in[j] = ends[0, j]
    for j in range(2):
        out_a_in[4 + j] = ends[1, j]
        out_res[j] = ends[1, 2 + j]
    box.drain()


def tail(mixer, tokens, grads, wide, thin):
    model = tokens[2].shape[1]
    count, inner = mixer[-1].shape
    heads = inner // DH
    share = model // 4
    ff = grads[3].shape[1]

    def half_of(width):
        return -(-width // 256) * 128

    half, early_half = half_of(3 * inner + 128), half_of(3 * ff + inner)
    vmem = pl.BlockSpec(memory_space=pltpu.VMEM)
    anywhere = pl.BlockSpec(memory_space=pl.ANY)
    copies = 3 + 3 + 3 + 3 + 4 * 7 + 2 + 6
    results = [
        (count, share), (6, model // 128, 128), (3, 4, inner), (4, heads),
        (4, inner), (2, 4, ff), (4, ff), (2, model // 128, 128),
    ]
    scratch = [
        ((model, 3 * inner + 128), NARROW),
        ((model, 512), NARROW),
        ((3, HALO + count, inner), WIDE),
        ((HALO + count, 3 * inner), WIDE),
        ((3, 8, inner), WIDE),
        ((count, 3 * inner), NARROW),
        ((4, count, 128), NARROW),
        ((4, count, share), NARROW),
        ((3, count, share), NARROW),
        ((3, count, 128), NARROW),
        ((8, count), WIDE),
        ((3, 8, count), WIDE),
        ((2, 8, half), WIDE),
        ((2, 8, early_half), WIDE),
        ((2, 4, model // 128, 128), WIDE),
    ]
    scratch += DpSum.scratch(32, half) + DpSum.scratch(model // 8, 128) + DpSum.scratch(model // 8, 128)
    scratch += DpSum.scratch(32, early_half)
    operands = (*mixer, *tokens, *grads)
    return pl.pallas_call(
        tail_kernel,
        out_shape=tuple(jax.ShapeDtypeStruct(r, WIDE) for r in results),
        in_specs=[vmem] * len(operands) + [anywhere] * 2,
        out_specs=tuple([vmem] * len(results)),
        scratch_shapes=[pltpu.VMEM(*s) for s in scratch]
        + [
            pltpu.SemaphoreType.DMA((copies,)),
            pltpu.SemaphoreType.DMA((copies,)),
            pltpu.SemaphoreType.DMA((2,)),
        ],
        compiler_params=pltpu.CompilerParams(
            collective_id=3, has_side_effects=True, vmem_limit_bytes=60 << 20
        ),
        name="tail",
    )(*operands, wide, thin)


def on_device(
    layer_in, cotangent, segments, adapters, norm_one, norm_two, out_gain, beta_bias, conv_taps,
    w_qkv, w_beta, w_out, w_gate_up, w_down, a_in, b_heads, b_beta, a_out, b_ffn, a_down, b_res,
):
    heads = w_beta.shape[1]
    inner = heads * DH
    ff = w_down.shape[0]

    def rows_of(vector, count=8):
        return jnp.broadcast_to(vector[None, :], (count, vector.shape[0]))

    def pack_ranks(parts, blocks):
        flat = jnp.concatenate(parts, axis=1).reshape(-1, 128)
        flat = jnp.pad(flat, ((0, 64 * blocks - flat.shape[0]), (0, 0)))
        return flat.reshape(blocks, 64, 128).transpose(1, 0, 2).reshape(64, blocks * 128)

    last = jnp.concatenate(
        [
            w_gate_up.reshape(64, 2 * ff),
            w_down.T,
            pack_ranks([b_ffn.transpose(1, 0, 2).reshape(4, 2 * ff), a_down.T], 3),
        ],
        axis=1,
    )
    last = lax.all_gather(last, "dp", axis=0, tiled=True)
    beta = jnp.concatenate([w_beta, jnp.zeros((64, 64 - heads), NARROW), jnp.pad(b_beta, ((0, 60), (0, 0)))], axis=1)
    wide = jnp.concatenate(
        [
            w_qkv.reshape(64, 3 * inner),
            jnp.pad(beta, ((0, 0), (8, 56 - heads))),
            pack_ranks([b_heads.transpose(1, 0, 2).reshape(4, 3 * inner), a_out.T], 1),
        ],
        axis=1,
    )
    a_flat = a_in.reshape(16, 768)
    late_thin = jnp.concatenate([a_flat[:, 512:], b_res.transpose(2, 0, 1).reshape(16, 256)], axis=1)
    seg_row = rows_of(segments.astype(WIDE))
    taps = jnp.pad(conv_taps.reshape(3 * KW, inner).astype(WIDE), ((0, 4), (0, 0)))
    (
        wide, thin, late, pre, aux, picks, xn_one, u_one, q, k, v, t_map, w_map, u_map, reach, ranks,
        maps, sib_a, chip_a, row_a, state_in, mixer_out, normed, u_out, branch, g_full,
    ) = front(
        layer_in, cotangent, seg_row, adapters, rows_of(norm_one), rows_of(out_gain),
        rows_of(jnp.pad(beta_bias, (8, 120 - heads))), taps, wide, a_flat[:, :512], w_out.T, late_thin,
    )
    wide, thin, late = (x.reshape(2048, -1) for x in (wide, thin, late))
    output, state_grad, d_hidden_one, d_mixer, grad_b_ffn, grad_a_down, grad_a_out, shared_two = middle(
        (maps, sib_a, chip_a, row_a), (reach, mixer_out, normed, u_out, branch, picks),
        layer_in, g_full, rows_of(norm_two), rows_of(out_gain), ranks, late, last,
    )
    grad_input, d_a_in, d_b_heads, d_b_beta, d_a_out, d_b_ffn, d_a_down, d_b_res = tail(
        (pre, taps, aux, seg_row, q, k, v, t_map, w_map, u_map, state_in, state_grad, d_mixer),
        (u_one, xn_one, layer_in, d_hidden_one, rows_of(norm_one), picks, ranks),
        (shared_two, grad_b_ffn, grad_a_out, grad_a_down),
        wide,
        thin,
    )
    return (
        output, grad_input, d_a_in.transpose(1, 0, 2), d_b_heads, d_b_beta, d_a_out.T, d_b_ffn, d_a_down.T,
        d_b_res.transpose(0, 2, 1),
    )


def solution(mesh):
    placed = (
        P("dp", None),
        P("dp", "mp"),
        P("dp"),
        P(),
        P(),
        P(),
        P(),
        P("mp"),
        P(None, None, "mp"),
        P("dp", None, "mp"),
        P("dp", "mp"),
        P("mp", "dp"),
        P("dp", None, "mp"),
        P("mp", "dp"),
        P(("dp", "mp"), None, None),
        P(None, "dp", "mp"),
        P("dp", "mp"),
        P("mp", "dp"),
        P(None, "dp", "mp"),
        P("mp", "dp"),
        P(None, None, ("dp", "mp")),
    )
    return jax.shard_map(
        on_device,
        mesh=mesh,
        in_specs=placed,
        out_specs=(
            P("dp", "mp"),
            P("dp", "mp"),
            P(("dp", "mp"), None, None),
            P(None, "dp", "mp"),
            P("dp", "mp"),
            P("mp", "dp"),
            P(None, "dp", "mp"),
            P("mp", "dp"),
            P(None, None, ("dp", "mp")),
        ),
        check_vma=False,
    )
```

profile of v0, /device:TPU:1, one launch (start us, length us, event | category | flops | bytes accessed | tf_op | source)
XLA Modules:
  0.0 294.1 jit_solution(14763785038039523506)
XLA Ops:
  7.4 0.9 pad_maximum_fusion.1
  8.3 1.0 copy.45
  9.3 1.8 pad_maximum_fusion
  11.2 0.6 slice.8.thin_ref
  12.2 0.6 pad_maximum_fusion.3.late_thin
  12.8 0.6 pad_convert_fusion.taps_ref
  13.5 0.8 fusion.3.wide_ref
  14.3 0.6 broadcast_in_dim.15.bias_ref
  14.9 0.6 broadcast_in_dim.14.gain_ref
  15.5 0.6 broadcast_in_dim.12.seg_ref
  16.1 0.6 broadcast_in_dim.13.norm_ref
  16.7 140.9 %front.1 = (bf16[32,64,1792]{2,1,0:T(8,128)(2,1)}, bf16[32,64,512]{2,1,0:T(8,128)(2,1)}, bf16[32,64,1024]{2,1,0:T(8,128)(2,1)}, bf16[272,1536]{1,0:T(8,128)(2,1)...) custom-call(bf16[256,2048]{1,0:T(8,128)(2,1)} %x_ref.5, ...), custom_call_target="tpu_custom_call" | custom-call | tf_op jit(solution)/shard_map/front/pallas_call | solution.py:728
  157.7 0.6 broadcast_in_dim.17.norm_ref
  158.3 68.5 %middle.1 = (bf16[256,512]{1,0:T(8,128)(2,1)}, f32[4,128,128]{2,1,0:T(8,128)}, f32[256,2048]{1,0:T(8,128)}, f32[256,512]{1,0:T(8,128)}, bf16[128,2816]{1,0:T(8,1...) custom-call(bf16[4,128,128]{2,1,0:T(8,128)(2,1)} %get-tuple-element.51.a_ref, ...), custom_call_target="tpu_custom_call" | custom-call | tf_op jit(solution)/shard_map/middle/pallas_call | solution.py:917
  226.8 48.2 %tail.1 = (f32[256,512]{1,0:T(8,128)}, f32[6,16,128]{2,1,0:T(8,128)}, f32[3,4,512]{2,1,0:T(4,128)}, f32[4,4]{1,0:T(4,128)}, f32[4,512]{1,0:T(4,128)}, /*index=5*...) custom-call(bf16[272,1536]{1,0:T(8,128)(2,1)} %get-tuple-element.65.pre_ref, ...), custom_call_target="tpu_custom_call" | custom-call | tf_op jit(solution)/shard_map/tail/pallas_call | solution.py:1199
  275.1 0.7 copy.59
  275.8 1.9 copy.60
  277.7 1.4 copy.61
  279.1 1.3 copy.62
  280.4 1.2 copy.63
  281.7 1.3 copy.64
  283.0 1.4 copy.65
  284.4 1.3 copy.66
  285.7 1.3 copy.67
  (48 shorter events, 0.6 us)
Async XLA Ops:
  7.2 4.0 %copy-start = (bf16[16,6,128]{2,0,1:T(8,128)(2,1)S(1)}, bf16[16,6,128]{2,0,1:T(8,128)(2,1)}, u32[]{:S(2)}) copy-start(bf16[16,6,128]{2,0,1:T(8,128)(2,1)} %param.35) | copy-start | bytes 73732
  7.2 4.6 %copy-start.11 = (s32[256]{0:T(256)S(1)}, s32[256]{0:T(256)}, u32[]{:S(2)}) copy-start(s32[256]{0:T(256)} %param.23) | copy-start | bytes 3076
  7.2 4.6 %copy-start.3 = (bf16[4,3,512]{2,0,1:T(4,128)(2,1)S(1)}, bf16[4,3,512]{2,0,1:T(4,128)(2,1)}, u32[]{:S(2)}) copy-start(bf16[4,3,512]{2,0,1:T(4,128)(2,1)} %param.29) | copy-start | bytes 36868
  7.2 4.6 %copy-start.9 = (bf16[64,4]{0,1:T(4,128)(2,1)S(1)}, bf16[64,4]{0,1:T(4,128)(2,1)}, u32[]{:S(2)}) copy-start(bf16[64,4]{0,1:T(4,128)(2,1)} %param.31) | copy-start | bytes 1540
  7.2 4.7 %copy-start.8 = (bf16[512,4]{0,1:T(4,128)(2,1)S(1)}, bf16[512,4]{0,1:T(4,128)(2,1)}, u32[]{:S(2)}) copy-start(bf16[512,4]{0,1:T(4,128)(2,1)} %param.38) | copy-start | bytes 12292
  7.2 4.7 %copy-start.4 = (bf16[3,4,512]{2,1,0:T(4,128)(2,1)S(1)}, bf16[3,4,512]{2,1,0:T(4,128)(2,1)}, u32[]{:S(2)}) copy-start(bf16[3,4,512]{2,1,0:T(4,128)(2,1)} %param.36) | copy-start | bytes 36868
  7.2 4.8 %copy-start.2 = (bf16[64,3,512]{2,0,1:T(8,128)(2,1)S(1)}, bf16[64,3,512]{2,0,1:T(8,128)(2,1)}, u32[]{:S(2)}) copy-start(bf16[64,3,512]{2,0,1:T(8,128)(2,1)} %param.30) | copy-start | bytes 589828
  7.3 4.8 %copy-start.13 = (f32[4]{0:T(128)S(1)}, f32[4]{0:T(128)}, u32[]{:S(2)}) copy-start(f32[4]{0:T(128)} %param.28) | copy-start | bytes 52
  7.3 4.9 %copy-start.7 = (bf16[2,128,16]{1,2,0:T(8,128)(2,1)S(1)}, bf16[2,128,16]{1,2,0:T(8,128)(2,1)}, u32[]{:S(2)}) copy-start(bf16[2,128,16]{1,2,0:T(8,128)(2,1)} %param.41) | copy-start | bytes 24580
  7.3 6.2 %copy-start.10 = (bf16[4,4]{1,0:T(4,128)(2,1)S(1)}, bf16[4,4]{1,0:T(4,128)(2,1)}, u32[]{:S(2)}) copy-start(bf16[4,4]{1,0:T(4,128)(2,1)} %param.37) | copy-start | bytes 100
  7.3 7.6 %copy-start.12 = (f32[128]{0:T(128)S(1)}, f32[128]{0:T(128)}, u32[]{:S(2)}) copy-start(f32[128]{0:T(128)} %param.27) | copy-start | bytes 1540
  7.3 8.8 %copy-start.5 = (f32[2048]{0:T(1024)S(1)}, f32[2048]{0:T(1024)}, u32[]{:S(2)}) copy-start(f32[2048]{0:T(1024)} %param.25) | copy-start | bytes 24580
  7.3 150.4 %all-gather.2.cloned.1.call-start = ((), (), s32[]{:S(2)}) async-start(), calls=%async_computation | async-start | bytes 19464192 | tf_op jit(solution)/shard_map/all_gather | solution.py:1241
  11.1 146.6 %copy-start.6 = (f32[2048]{0:T(1024)S(1)}, f32[2048]{0:T(1024)}, u32[]{:S(2)}) copy-start(f32[2048]{0:T(1024)} %param.26) | copy-start | bytes 24580
  226.8 48.3 %copy-start.1 = (bf16[256,512]{1,0:T(8,128)(2,1)S(1)}, bf16[256,512]{1,0:T(8,128)(2,1)}, u32[]{:S(2)}) copy-start(bf16[256,512]{1,0:T(8,128)(2,1)} %get-tuple-element.102) | copy-start | bytes 786436
Sparse Core Ops, SparseCore 0:
  11.3 106.5 all-gather.1
where the time goes:
time: 298 us; the launch traced here: 294 us
  Pallas kernels  258 us (87%)
  local copies, waits for them, and re-layouts  17.1 us (6%)
  between operations  14.5 us (5%)
  other arithmetic  4.75 us (2%)
    pallas_call x1, Pallas kernels, front(): pl.pallas_call(front_kernel, out_shape=tuple((jax.ShapeDtypeStruct(*r) fo...  141 us
    pallas_call x1, Pallas kernels, middle(): pl.pallas_call(middle_kernel, out_shape=tuple((jax.ShapeDtypeStruct(*r) f...  68.5 us
    pallas_call x1, Pallas kernels, tail(): pl.pallas_call(tail_kernel, out_shape=tuple((jax.ShapeDtypeStruct(r, WIDE...  48.2 us
    unnamed x40, local copies, waits for them, and re-layouts  13.2 us
  transfers between devices with their start and end apart: 1, of which 0 were waited for; matrix products, arithmetic and copies ran while one was open for 2% of the time, Pallas kernels for 48%

commit v1 on v0

--- a/solution.py
+++ b/solution.py
@@ -190,6 +190,11 @@
         shifted = pre_ref[pl.ds(HALO - j, count), cols]
         total = total + shifted * aux[:, j : j + 1] * taps[3 * j + part : 3 * j + part + 1]
     return total
+
+
+def spread_taps(taps_ref, taps):
+    for j in range(KW):
+        taps[3 * j : 3 * j + 3, :] = taps_ref[j].astype(WIDE)
 
 
 def masks(aux, seg_row):
@@ -266,7 +271,7 @@
     tick()
 
 
-def mixer_backward(heads, pre_ref, taps_ref, aux, seg_row, kept, state_ref, grad_ref, d_out_ref, d_ext):
+def mixer_backward(heads, pre_ref, taps_ref, aux, seg_row, kept, state_ref, grad_ref, d_out_ref, d_ext, between):
     q_ref, k_ref, v_ref, t_ref, w_ref, u_ref = kept
     count = aux.shape[0]
     inner = d_out_ref.shape[1]
@@ -288,6 +293,7 @@
     )
     d_right = each(lambda t, d: wide_dot(t, d, 0, 0), [t_ref[h] for h in heads], d_written)
     d_scores = each(lambda d, w: jnp.where(upto, wide_dot(d, w, 1, 1), 0.0), d_out, written)
+    between()
     d_lower = each(lambda d, w: jnp.where(below, -wide_dot(d, w, 1, 1), 0.0), d_right, written)
     d_q = each(
         lambda ds, b, d, s: wide_dot(ds, b) + linked * wide_dot(d, s, 1, 1), d_scores, k, d_out, state
@@ -471,25 +477,43 @@
         self.box, self.part, self.landed = box, part, landed
         self.m = lax.axis_index("mp")
         self.peers = {k: lax.rem(self.m + k, 4) for k in (1, 2, 3)}
-        self.copies = []
+        self.copies = ([], [])
+        self.half = part.shape[1] // 2
 
     def owner(self, k):
         return lax.rem(self.m + k, 4)
 
-    def send(self, k):
-        self.copies.append(self.box.push(self.part.at[k], self.landed.at[k - 1], mp=self.peers[k]))
-
-    def total(self):
-        for copy in self.copies:
+    def rows(self, half):
+        return pl.ds(half * self.half, self.half)
+
+    def send(self, k, half):
+        rows = self.rows(half)
+        self.copies[half].append(
+            self.box.push(self.part.at[k, rows], self.landed.at[k - 1, rows], mp=self.peers[k])
+        )
+
+    def send_half(self, half):
+        for k in self.ORDER:
+            self.send(k, half)
+
+    def total(self, half):
+        for copy in self.copies[half]:
             copy.wait_recv()
-        total = self.part[0].astype(WIDE)
+        rows = self.rows(half)
+        total = self.part[0, rows].astype(WIDE)
         for k in range(3):
-            total = total + self.landed[k].astype(WIDE)
+            total = total + self.landed[k, rows].astype(WIDE)
         return total
 
-    def share(self, out, width):
-        block = out.at[:, columns(self.m, width)]
-        return [self.box.push(block, block, mp=self.peers[k]) for k in self.ORDER]
+    def share(self, out):
+        width = self.part.shape[2]
+        shared = []
+        for half in range(2):
+            rows = self.rows(half)
+            out[rows, columns(self.m, width)] = self.total(half).astype(out.dtype)
+            block = out.at[rows, columns(self.m, width)]
+            shared += [self.box.push(block, block, mp=self.peers[k]) for k in self.ORDER]
+        return shared
 
 
 def unpack_ranks(block, spread, ranks, first, tiles):
@@ -502,11 +526,11 @@
 
 
 def front_kernel(
-    x_ref, g_own, seg_ref, adapters, norm_ref, gain_ref, bias_ref, taps_ref, wide_ref, thin_ref, late_ref, late_thin,
-    wide_out, thin_out, late_out, pre, aux_ref, picks_ref, xn_ref, u_ref, q_ref, k_ref, v_ref, t_ref, w_ref, u_map_ref,
-    reach, ranks, a_ref, sib_a, chip_a, row_a, state_out, mixer_out, normed, u_out_ref, branch, g_full,
-    wide_all, thin_all, late_all, thin_own, late_own, halo_x, seg_ext, xn_ext, pre_wide, block, spread, b_beta,
-    b_ref, out_zero, sib_b, chip_b, row_b, pass_on, part, landed, send, recv, local,
+    x_ref, seg_ref, adapters, norm_ref, gain_ref, bias_ref, taps_ref, wide_ref, thin_ref, late_ref, late_thin,
+    wide_out, thin_out, late_out, pre_out, xn_out, kept_out, t_out, aux_ref, picks_ref, u_ref,
+    reach, ranks, a_ref, sib_a, chip_a, row_a, state_out, mixer_out, normed, u_out_ref, branch,
+    pre, xn_ref, kept, t_ref, wide_all, thin_all, late_all, thin_own, late_own, halo_x, seg_ext, xn_ext, pre_wide, block, spread, b_beta,
+    b_ref, out_zero, sib_b, chip_b, row_b, pass_on, part, landed, taps, send, recv, local,
 ):
     count, model = x_ref.shape
     heads = a_ref.shape[0]
@@ -519,7 +543,8 @@
     chain = Chain(box, a_ref, sib_a, chip_a, row_a)
     greet([before, after] + chain.peers(), list(mp_peers.values()))
     me = moved(0, 0)
-    seg_ext[HALO:] = jnp.concatenate([seg_ref[...]] * 16, axis=0).T
+    seg_row = seg_ref[...].astype(WIDE)
+    seg_ext[HALO:] = jnp.broadcast_to(seg_row, (128, count)).T
     edges = [
         box.push(x_ref.at[pl.ds(count - HALO, HALO)], halo_x, dp=after),
         box.push(seg_ext.at[pl.ds(count, HALO)], seg_ext.at[pl.ds(0, HALO)], dp=after),
@@ -541,15 +566,13 @@
     thin_steps = gather_steps(box, thin_own, thin_all)
     late_steps = gather_steps(box, late_own, late_all)
     wide_steps.pop(0)()
-    share = g_own.shape[1]
-    g_full[:, columns(m, share)] = g_own[...]
+    share = model // 4
     keep[1].wait()
     for copy in crossing:
         copy.wait_recv()
     keep_thin = pltpu.make_async_copy(thin_own, thin_all.at[me], local.at[4])
     keep_thin.start()
     thin_steps.pop(0)()
-    g_sent = [box.push(g_own, g_full.at[:, columns(m, share)], mp=mp_peers[k]) for k in MpSum.ORDER]
 
     def normal(rows):
         rows = rows.astype(WIDE)
@@ -576,7 +599,7 @@
     for copy in to_hbm:
         copy.start()
 
-    def tick(steps=1):
+    def tick(steps):
         for _ in range(min(steps, len(late_steps))):
             late_steps.pop(0)()
 
@@ -584,6 +607,7 @@
         copy.wait_recv()
     xn_ext[:HALO] = normal(halo_x[...])
     seg_ext[:HALO] = jnp.where(place == 0, -1.0, seg_ext[:HALO])
+    spread_taps(taps_ref, taps)
     lanes = lax.broadcasted_iota(jnp.int32, seg_ext.shape, 1)
     seg_all = seg_ext[...]
     per_token = jnp.zeros(seg_all.shape, WIDE)
@@ -602,11 +626,11 @@
     beta_lane = lax.broadcasted_iota(jnp.int32, beta.shape, 1)
     beta = jnp.where((beta_lane >= 8) & (beta_lane < 8 + heads), beta, 0.0)
     ranks[:, 4 * inner :] = beta.astype(NARROW)
-    tick()
+    tick(1)
     u_ext = dot(xn_ext[...], thin_all[...].reshape(model, thin_all.shape[2]))
     u_ext = (u_ext * jnp.concatenate([picks_ext] * 4, axis=1)).astype(NARROW)
     u_ref[...] = u_ext[HALO:]
-    tick()
+    tick(1)
     for j in range(3):
         cols = slice(j * inner, (j + 1) * inner)
         value = dot(xn_ext[...], wide_all[:, :, cols].reshape(model, inner)) + dot(
@@ -615,11 +639,13 @@
         value = value.astype(NARROW)
         pre[:, cols] = value
         pre_wide[:, cols] = value.astype(WIDE)
-        tick()
+        tick(1)
     w_beta = wide_all[:, :, 3 * inner : 3 * inner + 128].reshape(model, 128)
-    logits = dot(xn_ref[...], w_beta) + dot(u_ref[:, 384:], ranks[:, 4 * inner :]) + bias_ref[0:1, :]
+    logits = dot(xn_ref[...], w_beta) + dot(u_ref[:, 384:], ranks[:, 4 * inner :])
     seg = seg_all[HALO:]
     lane = lanes[HALO:]
+    for h in range(heads):
+        logits = jnp.where(lane == 8 + h, logits + bias_ref[h], logits)
     aux = jnp.where((lane >= 8) & (lane < 8 + heads), jax.nn.sigmoid(logits), 0.0)
     for j in range(KW):
         aux = jnp.where((lane == j) & (seg_ext[pl.ds(HALO - j, count)] == seg), 1.0, aux)
@@ -627,19 +653,23 @@
     aux = jnp.where((lane == 5) & (seg == seg_ext[HALO + count - 1 : HALO + count]), 1.0, aux)
     aux = jnp.where(lane == 6, seg, aux)
     aux_ref[...] = aux
-    for first in range(0, heads, 2):
-        mixer_forward(
-            list(range(first, min(first + 2, heads))), pre_wide, taps_ref, aux, seg_ref[0:1, :],
-            out_zero, reach, a_ref, b_ref, (q_ref, k_ref, v_ref, t_ref, w_ref, u_map_ref), tick,
-        )
+    mixer_forward(
+        list(range(heads)), pre_wide, taps, aux, seg_row, out_zero, reach, a_ref, b_ref,
+        (*(kept.at[i] for i in range(3)), t_ref, *(kept.at[i] for i in (3, 4))), lambda: tick(2),
+    )
+    for i, (source, target) in enumerate(((pre, pre_out), (xn_ref, xn_out), (kept, kept_out), (t_ref, t_out))):
+        to_hbm.append(pltpu.make_async_copy(source, target, local.at[9 + i]))
+        to_hbm[-1].start()
     chain.start_forward(b_ref, sib_b, chip_b, row_b, pass_on)
+    tick(2)
+    chain.chips_forward()
+    tick(2)
+    chain.rows_forward()
     tick(len(late_steps))
+    chain.finish_forward(state_out)
     keep_late.wait()
     keep_late_out = pltpu.make_async_copy(late_all, late_out, local.at[8])
     keep_late_out.start()
-    chain.chips_forward()
-    chain.rows_forward()
-    chain.finish_forward(state_out)
     for h in range(heads):
         cols = slice(h * DH, (h + 1) * DH)
         rows = out_zero[:, cols] + wide_dot(reach[:, cols], state_out[h])
@@ -654,41 +684,41 @@
         b_mix = late_all[groups, :, inner + 256 : inner + 384].reshape(share, 128)
         part[k] = (dot_nt(normed[...], w_out) + dot_nt(u_out, b_mix)).astype(NARROW)
         if k:
-            one.send(k)
-    branch[:, columns(m, share)] = one.total().astype(NARROW)
-    for copy in g_sent + one.share(branch, share):
+            one.send(k, 0)
+    one.send_half(1)
+    for copy in one.share(branch):
         copy.wait_recv()
     for copy in to_hbm + [keep_late_out]:
         copy.wait()
     box.drain()
 
 
-def front(x, g, seg_row, adapters, norm, gain, bias, taps, wide, thin, late, late_thin):
+def front(x, seg_row, adapters, norm, gain, bias, taps, wide, thin, late, late_thin):
     count, model = x.shape
-    inner = taps.shape[1]
+    inner = taps.shape[2]
     heads = inner // DH
-    share = g.shape[1]
+    share = model // 4
     vmem = pl.BlockSpec(memory_space=pltpu.VMEM)
     anywhere = pl.BlockSpec(memory_space=pl.ANY)
+    smem = pl.BlockSpec(memory_space=pltpu.SMEM)
     two = (2, DH, DH)
     square = (heads, DH, DH)
     by_head = ((count, inner), WIDE)
     thin_all, late_all = (32, 64, thin.shape[1]), (32, 64, late.shape[1] + late_thin.shape[1])
+    early = [
+        ((HALO + count, 3 * inner), NARROW),
+        ((count, model), NARROW),
+        ((5, count, inner), WIDE),
+        ((heads, count, count), WIDE),
+    ]
     results = [
         ((32,) + wide.shape, NARROW),
         (thin_all, NARROW),
         (late_all, NARROW),
-        ((HALO + count, 3 * inner), NARROW),
+        *early,
         ((count, 128), WIDE),
         ((count, 128), WIDE),
-        ((count, model), NARROW),
         ((count, 512), NARROW),
-        by_head,
-        by_head,
-        by_head,
-        ((heads, count, count), WIDE),
-        by_head,
-        by_head,
         by_head,
         ((128, 4 * inner + 128), NARROW),
         (square, NARROW),
@@ -700,9 +730,8 @@
         ((count, inner), NARROW),
         ((count, 128), NARROW),
         ((count, model), NARROW),
-        ((count, model), NARROW),
     ]
-    scratch = [
+    scratch = early + [
         ((32,) + wide.shape, NARROW),
         (thin_all, NARROW),
         (late_all, NARROW),
@@ -723,24 +752,25 @@
         (two, WIDE),
         ((4, count, share), NARROW),
         ((3, count, share), NARROW),
+        ((16, inner), WIDE),
     ]
-    copies = 3 * GATHER_COPIES + 2 + 3 + 3 + 3 + 2 + 6 + 6 + 1 + 6
+    copies = 3 * GATHER_COPIES + 2 + 3 + 3 + 2 + 6 + 6 + 1 + 12
     return pl.pallas_call(
         front_kernel,
         out_shape=tuple(jax.ShapeDtypeStruct(*r) for r in results),
-        in_specs=[vmem] * 3 + [pl.BlockSpec(memory_space=pltpu.SMEM)] + [vmem] * 4 + [anywhere] * 4,
-        out_specs=tuple([anywhere] * 3 + [vmem] * (len(results) - 3)),
+        in_specs=[vmem] * 2 + [smem] + [vmem] * 2 + [smem, vmem] + [anywhere] * 4,
+        out_specs=tuple([anywhere] * 7 + [vmem] * (len(results) - 7)),
         scratch_shapes=[pltpu.VMEM(*s) for s in scratch]
         + [
             pltpu.SemaphoreType.DMA((copies,)),
             pltpu.SemaphoreType.DMA((copies,)),
-            pltpu.SemaphoreType.DMA((9,)),
+            pltpu.SemaphoreType.DMA((13,)),
         ],
         compiler_params=pltpu.CompilerParams(
             collective_id=0, has_side_effects=True, vmem_limit_bytes=60 << 20
         ),
         name="front",
-    )(x, g, seg_row, adapters, norm, gain, bias, taps, wide, thin, late, late_thin)
+    )(x, seg_row, adapters, norm, gain, bias, taps, wide, thin, late, late_thin)
 
 
 def middle_kernel(
@@ -786,13 +816,12 @@
     two_picks = jnp.concatenate([picks, picks], axis=1)
     loads[0].wait()
     u_two_ref[...] = (dot(xn_two[...], a_two[...]) * two_picks).astype(NARROW)
-    loads[1].wait()
+    for load in loads[1:4]:
+        load.wait()
     for i in range(3):
         block[i] = packed[:, i * 128 : (i + 1) * 128].astype(WIDE)
     unpack_ranks(block, spread, ranks, 0, 3 * ff // 128)
-    loads[2].wait()
     gate[...] = dot(xn_two[...], w_gu[:, :ff]) + dot(u_two_ref[:, :128], ranks[:, :ff])
-    loads[3].wait()
     up[...] = dot(xn_two[...], w_gu[:, ff:]) + dot(u_two_ref[:, 128:], ranks[:, ff : 2 * ff])
     hidden[...] = (gate[...] * jax.nn.sigmoid(gate[...]) * up[...]).astype(NARROW)
     loads[4].wait()
@@ -814,12 +843,12 @@
             dot_nt(d_gate_up[...], w_gu[rows, :]) + dot_nt(jnp.concatenate(e_two, axis=1), a_two[rows, :])
         ).astype(NARROW)
         if k:
-            two.send(k)
+            two.send(k, 0)
+    two.send_half(1)
     u_down = (dot_nt(hidden[...], a_down[...]) * picks).astype(NARROW)
     for j, value in enumerate((e_two[0], e_two[1], u_out, u_down)):
         extra[j] = value
-    d_xn[:, columns(m, share)] = two.total().astype(NARROW)
-    shared = two.share(d_xn, share)
+    shared = two.share(d_xn)
     extra_sent = [box.push(extra.at[mp_peers[k]], extra_landed.at[k - 1], mp=mp_peers[k]) for k in MpSum.ORDER]
     three = MpSum(box, ffn_part, ffn_landed)
     for k in (2, 1, 3, 0):
@@ -827,8 +856,8 @@
         ffn_part[k] = (dot_nt(hidden[...], w_down[rows, :]) + dot_nt(u_down, b_down[rows, :])).astype(NARROW)
     for copy in shared:
         copy.wait_recv()
-    for k in MpSum.ORDER:
-        three.send(k)
+    three.send_half(0)
+    three.send_half(1)
 
     rows = hidden_one[...]
     scale_two = inverse_rms(rows)
@@ -859,7 +888,9 @@
     left = jnp.where(m < 2, xn_two[...], jnp.where(m == 2, d_branch[...], g_full[...]))
     g_shared[...] = dot_tn(left, factor.astype(NARROW)).astype(NARROW)
     chain.finish_backward(grad_out)
-    output[...] = (hidden_one[:, columns(m, share)] + three.total()).astype(NARROW)
+    for half in range(2):
+        rows = three.rows(half)
+        output[rows] = (hidden_one[rows, columns(m, share)] + three.total(half)).astype(NARROW)
     box.drain()
 
 
@@ -873,7 +904,7 @@
     vmem = pl.BlockSpec(memory_space=pltpu.VMEM)
     anywhere = pl.BlockSpec(memory_space=pl.ANY)
     two = (2, DH, DH)
-    copies = 1 + 3 + 3 + 1 + 6 + 3 + 3
+    copies = 1 + 3 + 3 + 1 + 12 + 3 + 6
     results = [
         ((count, share), NARROW),
         ((heads, DH, DH), WIDE),
@@ -986,16 +1017,16 @@
 
 
 def tail_kernel(
-    pre_ref, taps_ref, aux_ref, seg_ref, q_ref, k_ref, v_ref, t_ref, w_ref, u_map_ref, state_ref, grad_ref, d_out_ref,
-    u_ref, xn_ref, x_ref, d_one_ref, norm_ref, picks_ref, ranks, shared_two, g_b_ffn, g_a_out, g_a_down,
-    wide_ref, thin_ref,
+    taps_ref, aux_ref, seg_ref, state_ref, grad_ref, d_out_ref,
+    u_ref, norm_ref, picks_ref, ranks, shared_two, g_b_ffn, g_a_out, g_a_down,
+    pre_in, kept_in, t_in, x_in, xn_in, d_one_in, wide_ref, thin_ref,
     grad_input, out_a_in, out_heads, out_beta, out_a_out, out_ffn, out_a_down, out_res,
-    w_in, a_one, d_ext, pre_wide, halo, d_pre, e_one, part, landed, extra_landed, sums, sums_landed, pair, early_pair, ends,
+    pre_ref, kept_all, t_ref, x_ref, xn_ref, d_one_ref, w_in, a_one, d_ext, pre_wide, taps, halo, d_pre, e_one, part, landed, extra_landed, sums, sums_landed, pair, early_pair, ends,
     *rest,
 ):
     one, two, three, four = (rest[i * DpSum.SCRATCH : (i + 1) * DpSum.SCRATCH] for i in range(4))
     send, recv, local = rest[4 * DpSum.SCRATCH :]
-    count, model = x_ref.shape
+    count, model = x_in.shape
     inner = d_out_ref.shape[1]
     heads = inner // DH
     ff = g_a_down.shape[1]
@@ -1005,6 +1036,23 @@
     mp_peers = {k: lax.rem(m + k, 4) for k in (1, 2, 3)}
     dp_peers = [before, after, moved(0, 0, True)]
     dp_peers += [moved(k, 0) for k in (1, 2, 3)] + [moved(0, k) for k in (1, 2, 3)]
+    loads = [
+        pltpu.make_async_copy(source, target, local.at[i])
+        for i, (source, target) in enumerate(
+            (
+                (pre_in, pre_ref),
+                (kept_in, kept_all),
+                (t_in, t_ref),
+                (wide_ref.at[:, pl.ds(0, w_in.shape[1])], w_in),
+                (thin_ref.at[:, pl.ds(0, a_one.shape[1])], a_one),
+                (x_in, x_ref),
+                (xn_in, xn_ref),
+                (d_one_in, d_one_ref),
+            )
+        )
+    ]
+    for load in loads:
+        load.start()
     greet(dp_peers, list(mp_peers.values()))
     box = Mailbox(send, recv)
     early_sum, heads_sum, two_sum, one_sum = (DpSum(box, *refs) for refs in (four, one, two, three))
@@ -1026,27 +1074,24 @@
     for i, value in enumerate(by_core(shared_two[...])):
         two[0][i] = value
     two_sum.over_cores()
-    loads = [
-        pltpu.make_async_copy(wide_ref.at[:, pl.ds(0, w_in.shape[1])], w_in, local.at[0]),
-        pltpu.make_async_copy(thin_ref.at[:, pl.ds(0, a_one.shape[1])], a_one, local.at[1]),
-    ]
-    for load in loads:
-        load.start()
     aux = aux_ref[...]
+    spread_taps(taps_ref, taps)
+    for load in loads[:3]:
+        load.wait()
     pre_wide[...] = pre_ref[...].astype(WIDE)
-    kept = (q_ref, k_ref, v_ref, t_ref, w_ref, u_map_ref)
+    kept = (*(kept_all.at[i] for i in range(3)), t_ref, *(kept_all.at[i] for i in (3, 4)))
     lanes = lax.broadcasted_iota(jnp.int32, aux.shape, 1)
     d_logit = jnp.zeros(aux.shape, WIDE)
-    for first in range(0, heads, 2):
-        some = list(range(first, min(first + 2, heads)))
-        found = mixer_backward(
-            some, pre_wide, taps_ref, aux, seg_ref[0:1, :], kept, state_ref, grad_ref, d_out_ref, d_ext
-        )
-        for h, value in zip(some, found):
-            d_logit = jnp.where(lanes == 8 + h, value, d_logit)
-        if first == 0:
-            early_sum.over_y()
-            two_sum.over_y()
+    def between():
+        early_sum.over_y()
+        two_sum.over_y()
+
+    found = mixer_backward(
+        list(range(heads)), pre_wide, taps, aux, seg_ref[...].astype(WIDE), kept, state_ref, grad_ref, d_out_ref, d_ext,
+        between,
+    )
+    for h, value in enumerate(found):
+        d_logit = jnp.where(lanes == 8 + h, value, d_logit)
     edges = [box.push(d_ext.at[i, pl.ds(HALO - 8, 8)], halo.at[i], dp=before) for i in range(3)]
     early_sum.over_z()
     two_sum.over_z()
@@ -1069,7 +1114,7 @@
     grads.append(dot_tn(u_ref[:, 384:], d_logit))
     halves(one, [value.astype(NARROW) for value in grads])
     heads_sum.over_cores()
-    for load in loads:
+    for load in loads[3:]:
         load.wait()
     share = grad_input.shape[1]
     total = MpSum(box, part, landed)
@@ -1085,7 +1130,8 @@
         )
         part[k] = value.astype(NARROW)
         if k:
-            total.send(k)
+            total.send(k, 0)
+            total.send(k, 1)
         weighted = value * norm_ref[0:1, rows] * x_ref[:, rows].astype(WIDE)
         row_sum = row_sum + jnp.sum(weighted, axis=1, keepdims=True)
     sums[...] = row_sum.T[:8]
@@ -1104,23 +1150,7 @@
     one_sum.over_cores()
     heads_sum.over_z()
     one_sum.over_y()
-    x_all = x_ref[...].astype(WIDE)
-    scale = inverse_rms(x_all)
-    mine = columns(m, share)
-    d_xn = total.total()
-    for copy in sums_sent:
-        copy.wait_recv()
-    rows = sums[...] + sums_landed[0] + sums_landed[1] + sums_landed[2]
-    mean = jnp.concatenate([rows] * 16, axis=0).T[:, :1] / model
-    grad_input[...] = d_one_ref[:, mine] + (
-        scale * norm_ref[0:1, mine] * d_xn - x_ref[:, mine].astype(WIDE) * (scale * scale * scale * mean)
-    )
-    heads_sum.finish()
-    pair[c] = one[5][...]
-    paired = box.push(one[5], pair.at[c], dp=moved(0, 0, True))
-    two_sum.finish()
     rank_rows = model // 128
-    one_sum.over_z()
 
     def to_owners(slot, result):
         ends[slot, m] = result[columns(m, rank_rows)]
@@ -1129,9 +1159,28 @@
             for k in MpSum.ORDER
         ]
 
+    two_sum.finish()
     owners = to_owners(1, two[5])
+    heads_sum.finish()
+    pair[c] = one[5][...]
+    paired = box.push(one[5], pair.at[c], dp=moved(0, 0, True))
+    one_sum.over_z()
+    x_all = x_ref[...].astype(WIDE)
+    scale = inverse_rms(x_all)
+    mine = columns(m, share)
     one_sum.finish()
     owners += to_owners(0, three[5])
+    for copy in sums_sent:
+        copy.wait_recv()
+    rows = sums[...] + sums_landed[0] + sums_landed[1] + sums_landed[2]
+    mean = jnp.concatenate([rows] * 16, axis=0).T[:, :1] / model
+    scale_three = scale * scale * scale * mean
+    for half in range(2):
+        at = total.rows(half)
+        here = slice(half * (count // 2), (half + 1) * (count // 2))
+        grad_input[at] = d_one_ref[at, mine] + (
+            scale[here] * norm_ref[0:1, mine] * total.total(half) - x_ref[at, mine].astype(WIDE) * scale_three[here]
+        )
     paired.wait_recv()
     early_paired.wait_recv()
 
@@ -1158,8 +1207,8 @@
     box.drain()
 
 
-def tail(mixer, tokens, grads, wide, thin):
-    model = tokens[2].shape[1]
+def tail(mixer, tokens, grads, kept, wide, thin):
+    model = kept[3].shape[1]
     count, inner = mixer[-1].shape
     heads = inner // DH
     share = model // 4
@@ -1171,16 +1220,17 @@
     half, early_half = half_of(3 * inner + 128), half_of(3 * ff + inner)
     vmem = pl.BlockSpec(memory_space=pltpu.VMEM)
     anywhere = pl.BlockSpec(memory_space=pl.ANY)
-    copies = 3 + 3 + 3 + 3 + 4 * 7 + 2 + 6
+    copies = 3 + 3 + 6 + 3 + 4 * 7 + 2 + 6
     results = [
         (count, share), (6, model // 128, 128), (3, 4, inner), (4, heads),
         (4, inner), (2, 4, ff), (4, ff), (2, model // 128, 128),
     ]
-    scratch = [
+    scratch = [(x.shape, x.dtype) for x in kept] + [
         ((model, 3 * inner + 128), NARROW),
         ((model, 512), NARROW),
         ((3, HALO + count, inner), WIDE),
         ((HALO + count, 3 * inner), WIDE),
+        ((16, inner), WIDE),
         ((3, 8, inner), WIDE),
         ((count, 3 * inner), NARROW),
         ((4, count, 128), NARROW),
@@ -1199,19 +1249,36 @@
     return pl.pallas_call(
         tail_kernel,
         out_shape=tuple(jax.ShapeDtypeStruct(r, WIDE) for r in results),
-        in_specs=[vmem] * len(operands) + [anywhere] * 2,
+        in_specs=[vmem] * len(operands) + [anywhere] * (len(kept) + 2),
         out_specs=tuple([vmem] * len(results)),
         scratch_shapes=[pltpu.VMEM(*s) for s in scratch]
         + [
             pltpu.SemaphoreType.DMA((copies,)),
             pltpu.SemaphoreType.DMA((copies,)),
-            pltpu.SemaphoreType.DMA((2,)),
+            pltpu.SemaphoreType.DMA((8,)),
         ],
         compiler_params=pltpu.CompilerParams(
             collective_id=3, has_side_effects=True, vmem_limit_bytes=60 << 20
         ),
         name="tail",
-    )(*operands, wide, thin)
+    )(*operands, *kept, wide, thin)
+
+
+def hand_over_kernel(*refs):
+    half = len(refs) // 2
+    for source, target in zip(refs[:half], refs[half:]):
+        target[...] = source[...]
+
+
+def hand_over(*arrays):
+    vmem = pl.BlockSpec(memory_space=pltpu.VMEM)
+    return pl.pallas_call(
+        hand_over_kernel,
+        out_shape=tuple(jax.ShapeDtypeStruct(x.shape, x.dtype) for x in arrays),
+        in_specs=[vmem] * len(arrays),
+        out_specs=tuple([vmem] * len(arrays)),
+        name="hand_over",
+    )(*arrays)
 
 
 def on_device(
@@ -1222,9 +1289,6 @@
     inner = heads * DH
     ff = w_down.shape[0]
 
-    def rows_of(vector, count=8):
-        return jnp.broadcast_to(vector[None, :], (count, vector.shape[0]))
-
     def pack_ranks(parts, blocks):
         flat = jnp.concatenate(parts, axis=1).reshape(-1, 128)
         flat = jnp.pad(flat, ((0, 64 * blocks - flat.shape[0]), (0, 0)))
@@ -1238,6 +1302,7 @@
         ],
         axis=1,
     )
+    g_full = lax.all_gather(cotangent, "mp", axis=1, tiled=True)
     last = lax.all_gather(last, "dp", axis=0, tiled=True)
     beta = jnp.concatenate([w_beta, jnp.zeros((64, 64 - heads), NARROW), jnp.pad(b_beta, ((0, 60), (0, 0)))], axis=1)
     wide = jnp.concatenate(
@@ -1250,26 +1315,29 @@
     )
     a_flat = a_in.reshape(16, 768)
     late_thin = jnp.concatenate([a_flat[:, 512:], b_res.transpose(2, 0, 1).reshape(16, 256)], axis=1)
-    seg_row = rows_of(segments.astype(WIDE))
-    taps = jnp.pad(conv_taps.reshape(3 * KW, inner).astype(WIDE), ((0, 4), (0, 0)))
+    seg_row = segments[None, :]
     (
-        wide, thin, late, pre, aux, picks, xn_one, u_one, q, k, v, t_map, w_map, u_map, reach, ranks,
-        maps, sib_a, chip_a, row_a, state_in, mixer_out, normed, u_out, branch, g_full,
+        wide, thin, late, pre, xn_one, kept, t_map, aux, picks, u_one, reach, ranks,
+        maps, sib_a, chip_a, row_a, state_in, mixer_out, normed, u_out, branch,
     ) = front(
-        layer_in, cotangent, seg_row, adapters, rows_of(norm_one), rows_of(out_gain),
-        rows_of(jnp.pad(beta_bias, (8, 120 - heads))), taps, wide, a_flat[:, :512], w_out.T, late_thin,
+        layer_in, seg_row, adapters, norm_one[None, :], out_gain[None, :],
+        beta_bias, conv_taps, wide, a_flat[:, :512], w_out.T, late_thin,
     )
     wide, thin, late = (x.reshape(2048, -1) for x in (wide, thin, late))
     output, state_grad, d_hidden_one, d_mixer, grad_b_ffn, grad_a_down, grad_a_out, shared_two = middle(
         (maps, sib_a, chip_a, row_a), (reach, mixer_out, normed, u_out, branch, picks),
-        layer_in, g_full, rows_of(norm_two), rows_of(out_gain), ranks, late, last,
+        layer_in, g_full, norm_two[None, :], out_gain[None, :], ranks, late, last,
     )
     grad_input, d_a_in, d_b_heads, d_b_beta, d_a_out, d_b_ffn, d_a_down, d_b_res = tail(
-        (pre, taps, aux, seg_row, q, k, v, t_map, w_map, u_map, state_in, state_grad, d_mixer),
-        (u_one, xn_one, layer_in, d_hidden_one, rows_of(norm_one), picks, ranks),
+        (conv_taps, aux, seg_row, state_in, state_grad, d_mixer),
+        (u_one, norm_one[None, :], picks, ranks),
         (shared_two, grad_b_ffn, grad_a_out, grad_a_down),
+        (pre, kept, t_map, layer_in, xn_one, d_hidden_one),
         wide,
         thin,
+    )
+    output, grad_input, d_a_in, d_b_heads, d_b_beta, d_a_out, d_b_ffn, d_a_down, d_b_res = hand_over(
+        output, grad_input, d_a_in, d_b_heads, d_b_beta, d_a_out, d_b_ffn, d_a_down, d_b_res
     )
     return (
         output, grad_input, d_a_in.transpose(1, 0, 2), d_b_heads, d_b_beta, d_a_out.T, d_b_ffn, d_a_down.T,

time: 298 us -> 262 us (0.88)
  Pallas kernels: 258 us -> 236 us
  local copies, waits for them, and re-layouts: 17.1 us -> 2.57 us
    pallas_call x1, Pallas kernels: 141 us -> 125 us  [front(): pl.pallas_call(front_kernel, out_shape=tuple((jax.ShapeDtypeStruct(*r) fo...]
    unnamed x40 -> x19, local copies, waits for them, and re-layouts: 13.2 us -> 1.79 us
    pallas_call x1, Pallas kernels: 48.2 us -> 41.4 us  [tail(): pl.pallas_call(tail_kernel, out_shape=tuple((jax.ShapeDtypeStruct(r, WIDE...]
    broadcast_in_dim x5 -> x0, local copies, waits for them, and re-layouts: 3.05 us -> none  [rows_of(): return jnp.broadcast_to(vector[None, :], (count, vector.shape[0]))]
  transfers between devices with their start and end apart: 1 -> 2, of which waited for: 0 -> 0; matrix products, arithmetic and copies ran while one was open for 2% -> 3% of each run, Pallas kernels for 48% -> 49%
where the time goes in v1:
time: 262 us; the launch traced here: 258 us
  Pallas kernels  236 us (90%)
  between operations  14.4 us (5%)
  other arithmetic  4.02 us (2%)
    pallas_call x1, Pallas kernels, front(): pl.pallas_call(front_kernel, out_shape=tuple((jax.ShapeDtypeStruct(*r) fo...  125 us
    pallas_call x1, Pallas kernels, middle(): pl.pallas_call(middle_kernel, out_shape=tuple((jax.ShapeDtypeStruct(*r) f...  67.2 us
    pallas_call x1, Pallas kernels, tail(): pl.pallas_call(tail_kernel, out_shape=tuple((jax.ShapeDtypeStruct(r, WIDE...  41.4 us
  transfers between devices with their start and end apart: 2, of which 0 were waited for; matrix products, arithmetic and copies ran while one was open for 3% of the time, Pallas kernels for 49%

profile of v1, /device:TPU:1, one launch (start us, length us, event | category | flops | bytes accessed | tf_op | source)
XLA Modules:
  0.0 257.8 jit_solution(16956708247339723001)
XLA Ops:
  7.2 0.0 copy-start
  7.2 0.0 copy-start.2
  7.2 0.0 copy-start.6
  7.2 0.0 copy-start.5
  7.3 0.0 all-gather.3.cloned.1.call-start
  7.3 0.7 all-gather.3.cloned.1.call-update
  8.0 0.0 all-gather.5.cloned.1.call-start
  8.0 0.8 pad_maximum_fusion.1
  8.9 1.0 copy.47
  9.9 1.8 pad_maximum_fusion
  11.7 0.0 all-gather.5.cloned.1.call-update
  11.8 0.6 slice.8.thin_ref
  12.4 0.6 copy.40.taps_ref
  13.0 0.1 copy.37
  13.2 0.1 pad.28.clone
  13.3 0.6 pad_maximum_fusion.3.late_thin
  13.9 0.1 fusion.5
  14.0 0.8 fusion.3.wide_ref
  14.7 125.2 %front.1 = (bf16[32,64,1792]{2,1,0:T(8,128)(2,1)}, bf16[32,64,512]{2,1,0:T(8,128)(2,1)}, bf16[32,64,1024]{2,1,0:T(8,128)(2,1)}, bf16[272,1536]{1,0:T(8,128)(2,1)...) custom-call(bf16[256,2048]{1,0:T(8,128)(2,1)} %x_in.1, ...), custom_call_target="tpu_custom_call" | custom-call | tf_op jit(solution)/shard_map/front/pallas_call | solution.py:758
  140.0 0.0 all-gather.3.cloned.1.call-done.g_full
  140.0 0.0 all-gather.5.cloned.1.call-done.wide_ref
  140.0 67.2 %middle.1 = (bf16[256,512]{1,0:T(8,128)(2,1)}, f32[4,128,128]{2,1,0:T(8,128)}, f32[256,2048]{1,0:T(8,128)}, f32[256,512]{1,0:T(8,128)}, bf16[128,2816]{1,0:T(8,1...) custom-call(bf16[4,128,128]{2,1,0:T(8,128)(2,1)} %get-tuple-element.55.a_ref, ...), custom_call_target="tpu_custom_call" | custom-call | tf_op jit(solution)/shard_map/middle/pallas_call | solution.py:948
  207.2 41.4 %tail.1 = (f32[256,512]{1,0:T(8,128)}, f32[6,16,128]{2,1,0:T(8,128)}, f32[3,4,512]{2,1,0:T(4,128)}, f32[4,4]{1,0:T(4,128)}, f32[4,512]{1,0:T(4,128)}, /*index=5*...) custom-call(bf16[4,3,512]{2,1,0:T(4,128)(2,1)} %copy.40.taps_ref, f32[256,128]{1,0:T(8,128)} %get-tuple-element.68.aux_ref, ...), custom_call_target="tpu_custom_call" | custom-call | tf_op jit(solution)/shard_map/tail/pallas_call | solution.py:1249
  248.7 2.1 hand_over.1
  (22 shorter events, 0.1 us)
Async XLA Ops:
  7.2 4.5 %copy-start = (bf16[16,6,128]{2,0,1:T(8,128)(2,1)S(1)}, bf16[16,6,128]{2,0,1:T(8,128)(2,1)}, u32[]{:S(2)}) copy-start(bf16[16,6,128]{2,0,1:T(8,128)(2,1)} %param.35) | copy-start | bytes 73732
  7.2 5.2 %copy-start.2 = (bf16[4,3,512]{2,0,1:T(4,128)(2,1)S(1)}, bf16[4,3,512]{2,0,1:T(4,128)(2,1)}, u32[]{:S(2)}) copy-start(bf16[4,3,512]{2,0,1:T(4,128)(2,1)} %param.29) | copy-start | bytes 36868
  7.2 5.8 %copy-start.6 = (bf16[64,4]{0,1:T(4,128)(2,1)S(1)}, bf16[64,4]{0,1:T(4,128)(2,1)}, u32[]{:S(2)}) copy-start(bf16[64,4]{0,1:T(4,128)(2,1)} %param.31) | copy-start | bytes 1540
  7.2 5.9 %copy-start.5 = (bf16[512,4]{0,1:T(4,128)(2,1)S(1)}, bf16[512,4]{0,1:T(4,128)(2,1)}, u32[]{:S(2)}) copy-start(bf16[512,4]{0,1:T(4,128)(2,1)} %param.38) | copy-start | bytes 12292
  7.2 5.9 %copy-start.3 = (bf16[3,4,512]{2,1,0:T(4,128)(2,1)S(1)}, bf16[3,4,512]{2,1,0:T(4,128)(2,1)}, u32[]{:S(2)}) copy-start(bf16[3,4,512]{2,1,0:T(4,128)(2,1)} %param.36) | copy-start | bytes 36868
  7.2 5.9 %copy-start.1 = (bf16[64,3,512]{2,0,1:T(8,128)(2,1)S(1)}, bf16[64,3,512]{2,0,1:T(8,128)(2,1)}, u32[]{:S(2)}) copy-start(bf16[64,3,512]{2,0,1:T(8,128)(2,1)} %param.30) | copy-start | bytes 589828
  7.2 6.0 %copy-start.4 = (bf16[2,128,16]{1,2,0:T(8,128)(2,1)S(1)}, bf16[2,128,16]{1,2,0:T(8,128)(2,1)}, u32[]{:S(2)}) copy-start(bf16[2,128,16]{1,2,0:T(8,128)(2,1)} %param.41) | copy-start | bytes 24580
  7.3 6.6 %copy-start.7 = (bf16[4,4]{1,0:T(4,128)(2,1)S(1)}, bf16[4,4]{1,0:T(4,128)(2,1)}, u32[]{:S(2)}) copy-start(bf16[4,4]{1,0:T(4,128)(2,1)} %param.37) | copy-start | bytes 100
  7.3 132.7 %all-gather.3.cloned.1.call-start = ((), (), s32[]{:S(2)}) async-start(), calls=%async_computation | async-start | bytes 1310720 | tf_op jit(solution)/shard_map/all_gather | solution.py:1305
  8.0 132.0 %all-gather.5.cloned.1.call-start = ((), (), s32[]{:S(2)}) async-start(), calls=%async_computation.1 | async-start | bytes 19464192 | tf_op jit(solution)/shard_map/all_gather | solution.py:1306
Sparse Core Ops, SparseCore 0:
  9.8 26.3 all-gather.2
  38.4 89.6 all-gather.4
